TPU v7x, 32 devices: a whole 2x2x4 slice. The times are simulated.
32 devices in a mesh: dp: 16 (over z, y, core), tensor: 2 (over x).
Axes of the slice: x: 2, y: 2, z: 4, core: 2. Of those that a mesh axis runs over, the one named last changes fastest.
Arguments:
- residual: bfloat16 [16384, 768], P(('dp', 'tensor')), may hold values from -6 to 6
- grad_out: bfloat16 [16384, 768], P(('dp', 'tensor')), may hold values from -6 to 6
- norm_gain: float32 [768], replicated, may hold values from 0.5 to 1.5
- w_zx: bfloat16 [2, 768, 1536], P(None, 'dp', 'tensor'), may hold values from -0.21875 to 0.21875
- w_dt: bfloat16 [768, 24], P('dp', 'tensor'), may hold values from -0.21875 to 0.21875
- w_bc: bfloat16 [2, 768, 128], P(None, 'dp'), may hold values from -0.21875 to 0.21875
- conv_x: float32 [4, 1536], P(None, 'tensor'), may hold values from -0.5 to 0.5
- conv_x_bias: float32 [1536], P('tensor'), may hold values from -0.5 to 0.5
- conv_bc: float32 [2, 4, 128], replicated, may hold values from -0.5 to 0.5
- conv_bc_bias: float32 [2, 128], replicated, may hold values from -0.5 to 0.5
- dt_bias: float32 [24], P('tensor'), may hold values from -6 to -2
- a_log: float32 [24], P('tensor'), may hold values from 0 to 2.77
- d_skip: float32 [24], P('tensor'), may hold values from 0.5 to 2
- gate_gain: float32 [1536], P('tensor'), may hold values from 0.5 to 1.5
- w_out: bfloat16 [1536, 768], P('tensor', 'dp'), may hold values from -0.15625 to 0.15625
Outputs:
- layer_out: bfloat16 [16384, 768], P(('dp', 'tensor'))
- d_residual: bfloat16 [16384, 768], P(('dp', 'tensor'))
- g_norm_gain: float32 [768], replicated
- g_w_zx: float32 [2, 768, 1536], P(None, 'dp', 'tensor')
- g_w_dt: float32 [768, 24], P('dp', 'tensor')
- g_w_bc: float32 [2, 768, 128], P(None, 'dp')
- g_conv_x: float32 [4, 1536], P(None, 'tensor')
- g_conv_x_bias: float32 [1536], P('tensor')
- g_conv_bc: float32 [2, 4, 128], replicated
- g_conv_bc_bias: float32 [2, 128], replicated
- g_dt_bias: float32 [24], P('tensor')
- g_a_log: float32 [24], P('tensor')
- g_d_skip: float32 [24], P('tensor')
- g_gate_gain: float32 [1536], P('tensor')
- g_w_out: float32 [1536, 768], P('tensor', 'dp')
All inputs are finite; a program needn't handle non-finite values.
Results may differ from a plain program's by a relative error of at most 0.0088.
Values may be sent and summed in bfloat16 or wider, within the bound.
A program may use at most 256 MiB of HBM per device.

v0:
```python
import jax
import jax.numpy as jnp
from jax import lax
from jax.sharding import PartitionSpec as P

Q = 256


EPS = 1e-05
HIGH = lax.Precision.HIGHEST
CONTRACT_LAST = (((1,), (1,)), ((), ()))
CONTRACT_FIRST = (((0,), (0,)), ((), ()))


def causal_conv(sequence, kernel, conv_bias):
    taps = kernel.shape[0]
    padded = jnp.pad(sequence, ((taps - 1, 0), (0, 0)))
    summed = jnp.zeros_like(sequence) + conv_bias[None, :]
    for offset in range(taps):
        summed = summed + kernel[offset][None, :] * padded[offset : offset + sequence.shape[0]]
    return summed


def conv_piece(projected, kernel, conv_bias):
    return jax.nn.silu(causal_conv(projected, kernel, conv_bias))


def ssd_block(memory, pieces):
    signal, inject, readout, timestep, decays = pieces
    running = jnp.cumsum(decays, axis=0)
    row_index = jnp.arange(signal.shape[0])
    causal_mask = (row_index[:, None] >= row_index[None, :])[:, :, None]
    weights = jnp.exp(jnp.where(causal_mask, running[:, None, :] - running[None, :, :], -jnp.inf))
    affinity = jnp.dot(readout, inject.T, precision=HIGH)
    mixing = affinity[:, :, None] * weights * timestep[None, :, :]
    within = jnp.einsum("ijh,jhp->ihp", mixing, signal, precision=HIGH)
    across = jnp.exp(running)[:, :, None] * jnp.einsum(
        "hpn,in->ihp", memory, readout, precision=HIGH
    )
    to_end = jnp.exp(running[-1][None, :] - running) * timestep
    carried = jnp.exp(running[-1])[:, None, None] * memory + jnp.einsum(
        "jh,jhp,jn->hpn", to_end, signal, inject, precision=HIGH
    )
    return (carried, within + across)


def ssd_local(signal, inject, readout, dt_raw, dt_bias, a_log, d_skip):
    length, channels = signal.shape
    head_count = dt_bias.shape[0]
    head_size = channels // head_count
    timestep = jax.nn.softplus(dt_raw + dt_bias)
    decays = -timestep * jnp.exp(a_log)

    def by_block(array):
        return array.reshape((length // Q, Q) + array.shape[1:])

    initial = jnp.zeros((head_count, head_size, inject.shape[1]), jnp.float32)
    heads_in = signal.reshape(length, head_count, head_size)
    _, outputs = lax.scan(
        ssd_block,
        initial,
        (
            by_block(heads_in),
            by_block(inject),
            by_block(readout),
            by_block(timestep),
            by_block(decays),
        ),
    )
    return outputs.reshape(length, channels) + jnp.repeat(d_skip, head_size) * signal


def body(
    residual,
    grad_out,
    norm_gain,
    w_zx,
    w_dt,
    w_bc,
    conv_x,
    conv_x_bias,
    conv_bc,
    conv_bc_bias,
    dt_bias,
    a_log,
    d_skip,
    gate_gain,
    w_out,
):
    full_zx, full_dt, full_bc, full_out = (
        lax.all_gather(w_zx, "dp", axis=1, tiled=True),
        lax.all_gather(w_dt, "dp", axis=0, tiled=True),
        lax.all_gather(w_bc, "dp", axis=1, tiled=True),
        lax.all_gather(w_out, "dp", axis=1, tiled=True),
    )
    own_rows = residual.shape[0]
    channels = gate_gain.shape[0]
    all_channels = channels * lax.axis_size("tensor")
    state_size = w_bc.shape[2]
    float_residual = residual.astype(jnp.float32)
    in_scale = lax.rsqrt(jnp.mean(float_residual * float_residual, axis=1, keepdims=True) + EPS)
    normed_own = (float_residual * in_scale * norm_gain).astype(jnp.bfloat16)
    normed = lax.all_gather(normed_own, "tensor", axis=0, tiled=True)
    gate_pre = jnp.dot(normed, full_zx[0], preferred_element_type=jnp.float32)
    joined_weight = jnp.concatenate([full_zx[1], full_bc[0], full_bc[1]], axis=1)
    projected = jnp.dot(normed, joined_weight, preferred_element_type=jnp.float32)
    dt_raw = jnp.dot(normed, full_dt, preferred_element_type=jnp.float32)
    kernel = jnp.concatenate([conv_x, conv_bc[0], conv_bc[1]], axis=1)
    kernel_bias = jnp.concatenate([conv_x_bias, conv_bc_bias[0], conv_bc_bias[1]])
    activated, conv_back = jax.vjp(conv_piece, projected, kernel, kernel_bias)
    rounded = lax.optimization_barrier(activated.astype(jnp.bfloat16)).astype(jnp.float32)
    signal = rounded[:, :channels]
    inject = rounded[:, channels : channels + state_size]
    readout = rounded[:, channels + state_size :]
    mixed, ssd_back = jax.vjp(ssd_local, signal, inject, readout, dt_raw, dt_bias, a_log, d_skip)
    gate_act = jax.nn.silu(gate_pre)
    gated_in = mixed * gate_act
    squares = lax.psum(jnp.sum(gated_in * gated_in, axis=1), "tensor")
    out_scale = lax.rsqrt(squares / all_channels + EPS)[:, None]
    gated = (gated_in * out_scale * gate_gain).astype(jnp.bfloat16)
    branch = lax.psum_scatter(
        jnp.dot(gated, full_out, preferred_element_type=jnp.float32),
        "tensor",
        scatter_dimension=0,
        tiled=True,
    )
    layer_out = (float_residual + branch).astype(jnp.bfloat16)
    cotangent = lax.all_gather(grad_out, "tensor", axis=0, tiled=True)
    d_gated = lax.dot_general(
        cotangent, full_out, CONTRACT_LAST, preferred_element_type=jnp.float32
    )
    grad_w_out = lax.dot_general(
        gated, cotangent, CONTRACT_FIRST, preferred_element_type=jnp.float32
    )
    scaled_grad = d_gated * gate_gain
    grad_gate_gain = jnp.sum(d_gated * gated_in * out_scale, axis=0)
    projection = lax.psum(jnp.sum(scaled_grad * gated_in, axis=1), "tensor")
    d_inner = out_scale * scaled_grad - gated_in * out_scale**3 * projection[:, None] / all_channels
    d_mixed = d_inner * gate_act
    logistic = jax.nn.sigmoid(gate_pre)
    d_gate = (d_inner * mixed * logistic * (1.0 + gate_pre * (1.0 - logistic))).astype(jnp.bfloat16)
    d_signal, d_inject, d_readout, d_dt_raw, grad_dt_bias, grad_a_log, grad_d_skip = ssd_back(
        d_mixed
    )
    d_projected, grad_kernel, grad_kernel_bias = conv_back(
        jnp.concatenate([d_signal, d_inject, d_readout], axis=1)
    )
    d_shared = lax.psum(d_projected[:, channels:], "tensor").astype(jnp.bfloat16)
    d_signal_low = d_projected[:, :channels].astype(jnp.bfloat16)
    d_dt_low = d_dt_raw.astype(jnp.bfloat16)
    first_row = lax.axis_index("tensor") * own_rows
    shared_own = lax.dynamic_slice_in_dim(d_shared, first_row, own_rows, 0)
    summed = lax.dot_general(d_gate, full_zx[0], CONTRACT_LAST, preferred_element_type=jnp.float32)
    summed = summed + lax.dot_general(
        d_signal_low, full_zx[1], CONTRACT_LAST, preferred_element_type=jnp.float32
    )
    d_normed = lax.psum_scatter(
        summed
        + lax.dot_general(d_dt_low, full_dt, CONTRACT_LAST, preferred_element_type=jnp.float32),
        "tensor",
        scatter_dimension=0,
        tiled=True,
    )
    shared_weight = jnp.concatenate([full_bc[0], full_bc[1]], axis=1)
    d_normed = d_normed + lax.dot_general(
        shared_own, shared_weight, CONTRACT_LAST, preferred_element_type=jnp.float32
    )
    grad_w_zx = jnp.stack(
        [
            lax.dot_general(normed, d_gate, CONTRACT_FIRST, preferred_element_type=jnp.float32),
            lax.dot_general(
                normed, d_signal_low, CONTRACT_FIRST, preferred_element_type=jnp.float32
            ),
        ]
    )
    grad_w_dt = lax.dot_general(
        normed, d_dt_low, CONTRACT_FIRST, preferred_element_type=jnp.float32
    )
    grad_shared = lax.dot_general(
        normed_own, shared_own, CONTRACT_FIRST, preferred_element_type=jnp.float32
    )
    grad_w_bc = jnp.stack([grad_shared[:, :state_size], grad_shared[:, state_size:]])
    grad_conv_bc = jnp.stack(
        [grad_kernel[:, channels : channels + state_size], grad_kernel[:, channels + state_size :]]
    )
    grad_conv_bc_bias = jnp.stack(
        [
            grad_kernel_bias[channels : channels + state_size],
            grad_kernel_bias[channels + state_size :],
        ]
    )
    weighted = d_normed * norm_gain
    grad_norm_gain = jnp.sum(d_normed * float_residual * in_scale, axis=0)
    d_residual = (
        grad_out.astype(jnp.float32)
        + in_scale * weighted
        - float_residual * in_scale**3 * jnp.mean(weighted * float_residual, axis=1, keepdims=True)
    )
    d_residual = d_residual.astype(jnp.bfloat16)
    shared = (grad_w_bc, grad_norm_gain, grad_conv_bc, grad_conv_bc_bias)
    shared = lax.psum((shared[0], shared[1], shared[2], shared[3]), "tensor")
    sum_zx, sum_dt, sum_out, sum_bc = (
        lax.psum_scatter(grad_w_zx, "dp", scatter_dimension=1, tiled=True),
        lax.psum_scatter(grad_w_dt, "dp", scatter_dimension=0, tiled=True),
        lax.psum_scatter(grad_w_out, "dp", scatter_dimension=1, tiled=True),
        lax.psum_scatter(shared[0], "dp", scatter_dimension=1, tiled=True),
    )
    reduced_small = lax.psum(
        (
            grad_kernel[:, :channels],
            grad_kernel_bias[:channels],
            grad_dt_bias,
            grad_a_log,
            grad_d_skip,
            grad_gate_gain,
            shared[1],
            shared[2],
            shared[3],
        ),
        "dp",
    )
    sum_norm = reduced_small[6]
    sum_conv_bc = reduced_small[7]
    sum_conv_bc_bias = reduced_small[8]
    return (
        layer_out,
        d_residual,
        sum_norm,
        sum_zx,
        sum_dt,
        sum_bc,
        reduced_small[0],
        reduced_small[1],
        sum_conv_bc,
        sum_conv_bc_bias,
        reduced_small[2],
        reduced_small[3],
        reduced_small[4],
        reduced_small[5],
        sum_out,
    )


def solution(mesh):
    in_specs = (
        P(("dp", "tensor"), None),
        P(("dp", "tensor"), None),
        P(),
        P(None, "dp", "tensor"),
        P("dp", "tensor"),
        P(None, "dp", None),
        P(None, "tensor"),
        P("tensor"),
        P(),
        P(),
        P("tensor"),
        P("tensor"),
        P("tensor"),
        P("tensor"),
        P("tensor", "dp"),
    )
    out_specs = (
        P(("dp", "tensor"), None),
        P(("dp", "tensor"), None),
        P(),
        P(None, "dp", "tensor"),
        P("dp", "tensor"),
        P(None, "dp", None),
        P(None, "tensor"),
        P("tensor"),
        P(),
        P(),
        P("tensor"),
        P("tensor"),
        P("tensor"),
        P("tensor"),
        P("tensor", "dp"),
    )
    return jax.shard_map(body, mesh=mesh, in_specs=in_specs, out_specs=out_specs, check_vma=False)
```

profile of v0, /device:TPU:0, one launch (start us, length us, event | category | flops | bytes accessed | tf_op | source)
XLA Modules:
  0.0 946.4 jit_solution(7063388835048321204)
XLA Ops:
  14.4 24.2 %all_gather.21 = bf16[2,768,128]{2,1,0:T(8,128)(2,1)S(1)} all-gather(bf16[2,48,128]{2,1,0:T(8,128)(2,1)S(1)} %copy-done.56), channel_id=1, replica_groups=mesh['dp'=16,'tensor'=2] {'dp'}, dimensions={1}, use_global_device_ids=true | all-gather | bytes 417792 | tf_op jit(solution)/shard_map/all_gather | solution.py:93
  38.8 17.7 %all-gather = bf16[16,48,12]{1,2,0:T(8,128)(2,1)S(1)} all-gather(bf16[1,48,12]{1,2,0:T(8,128)(2,1)S(1)} %bitcast.512), channel_id=1, replica_groups=mesh['dp'=16,'tensor'=2] {'dp'}, dimensions={0}, use_global_device_ids=true | all-gather | bytes 19584 | tf_op jit(solution)/shard_map/all_gather | solution.py:92
  59.7 27.1 %all-gather.8.cloned.1.call-done = bf16[2,768,768]{2,1,0:T(8,128)(2,1)} async-done(((bf16[2,48,768]{2,1,0:T(8,128)(2,1)}), bf16[2,768,768]{2,1,0:T(8,128)(2,1)}) %all-gather.8.cloned.1.call-update) | async-done | bytes 2359312 | tf_op jit(solution)/shard_map/all_gather | solution.py:91
  112.6 159.0 %while.71 = (s32[]{:T(128)}, f32[12,64,128]{2,1,0:T(8,128)S(1)}, f32[4,256,12,64]{1,0,3,2:T(4,128)}, f32[4,256,256,12]{2,1,3,0:T(8,128)}, f32[4,128,256]{1,2,0:T...) while((s32[]{:T(128)}, f32[12,64,128]{2,1,0:T(8,128)S(1)}, ...), condition=%wide.region_4.5_spmd.clone.clone, body=%wide.region_1.4_spmd.clone.clone.sunk | while | flops 1316591616 | bytes 23374272 | solution.py:59
  127.0 17.9 %dynamic_update_slice.221 = f32[4,256,12,64]{1,0,3,2:T(4,128)} dynamic-update-slice(f32[4,256,12,64]{1,0,3,2:T(4,128)} %get-tuple-element.1863, f32[1,256,12,64]{1,0,3,2:T(1,128)S(1)} %copy.263, s32[]{:T(128)} %get-tuple-element.1861, s32[]{:T(128)} %constant.172.clone.1..sunk.1, s32[]{:T(128)} %constant.172.clone.1..sunk.1, s32[]{:T(128)} %constant.172.clone.1..sunk.1) | dynamic-update-slice | bytes 1572868 | tf_op jit(solution)/shard_map/jvp()/while/body/jit(dynamic_update_index_in_dim)/dynamic_update_slice | solution.py:59
  166.7 17.9 %dynamic_update_slice.221 = f32[4,256,12,64]{1,0,3,2:T(4,128)} dynamic-update-slice(f32[4,256,12,64]{1,0,3,2:T(4,128)} %get-tuple-element.1863, f32[1,256,12,64]{1,0,3,2:T(1,128)S(1)} %copy.263, s32[]{:T(128)} %get-tuple-element.1861, s32[]{:T(128)} %constant.172.clone.1..sunk.1, s32[]{:T(128)} %constant.172.clone.1..sunk.1, s32[]{:T(128)} %constant.172.clone.1..sunk.1) | dynamic-update-slice | bytes 1572868 | tf_op jit(solution)/shard_map/jvp()/while/body/jit(dynamic_update_index_in_dim)/dynamic_update_slice | solution.py:59
  206.5 17.9 %dynamic_update_slice.221 = f32[4,256,12,64]{1,0,3,2:T(4,128)} dynamic-update-slice(f32[4,256,12,64]{1,0,3,2:T(4,128)} %get-tuple-element.1863, f32[1,256,12,64]{1,0,3,2:T(1,128)S(1)} %copy.263, s32[]{:T(128)} %get-tuple-element.1861, s32[]{:T(128)} %constant.172.clone.1..sunk.1, s32[]{:T(128)} %constant.172.clone.1..sunk.1, s32[]{:T(128)} %constant.172.clone.1..sunk.1) | dynamic-update-slice | bytes 1572868 | tf_op jit(solution)/shard_map/jvp()/while/body/jit(dynamic_update_index_in_dim)/dynamic_update_slice | solution.py:59
  246.3 17.9 %dynamic_update_slice.221 = f32[4,256,12,64]{1,0,3,2:T(4,128)} dynamic-update-slice(f32[4,256,12,64]{1,0,3,2:T(4,128)} %get-tuple-element.1863, f32[1,256,12,64]{1,0,3,2:T(1,128)S(1)} %copy.263, s32[]{:T(128)} %get-tuple-element.1861, s32[]{:T(128)} %constant.172.clone.1..sunk.1, s32[]{:T(128)} %constant.172.clone.1..sunk.1, s32[]{:T(128)} %constant.172.clone.1..sunk.1) | dynamic-update-slice | bytes 1572868 | tf_op jit(solution)/shard_map/jvp()/while/body/jit(dynamic_update_index_in_dim)/dynamic_update_slice | solution.py:59
  276.9 15.7 %copy.146 = f32[1024,768]{1,0:T(8,128)} copy(f32[1024,768]{0,1:T(8,128)S(1)} %bitcast.479) | data formatting | bytes 6291456 | tf_op jit(solution)/shard_map/jvp()/reshape | solution.py:70
  292.6 7.1 multiply_reduce_fusion.7
  299.7 5.5 psum.112
  306.4 5.6 multiply_reduce_fusion.4
  312.1 5.6 psum.113
  317.7 8.4 multiply_reduce_fusion.5
  338.2 223.9 %while.70 = (s32[]{:T(128)}, f32[12,64,128]{2,1,0:T(8,128)S(1)}, f32[4,256,12,64]{1,0,3,2:T(4,128)}, f32[4,256,128]{2,1,0:T(8,128)S(1)}, f32[4,256,128]{2,1,0:T(...) while((s32[]{:T(128)}, f32[12,64,128]{2,1,0:T(8,128)S(1)}, ...), condition=%wide.region_20.21_spmd.clone, body=%wide.region_10.20_spmd.clone.sunk | while | flops 2627893248 | bytes 29932224 | solution.py:59
  342.7 6.8 fusion.239
  366.5 17.9 %dynamic_update_slice.208 = f32[4,256,12,64]{1,0,3,2:T(4,128)} dynamic-update-slice(f32[4,256,12,64]{1,0,3,2:T(4,128)} %get-tuple-element.1949, f32[1,256,12,64]{1,0,3,2:T(1,128)S(1)} %copy.251, s32[]{:T(128)S(6)} %sub.193, s32[]{:T(128)} %constant.172.clone.1..sunk, s32[]{:T(128)} %constant.172.clone.1..sunk, s32[]{:T(128)} %constant.172.clone.1..sunk) | dynamic-update-slice | bytes 1572868 | tf_op jit(solution)/shard_map/transpose(jvp())/while/body/jit(dynamic_update_index_in_dim)/dynamic_update_slice | solution.py:59
  398.5 6.8 fusion.239
  422.3 17.9 %dynamic_update_slice.208 = f32[4,256,12,64]{1,0,3,2:T(4,128)} dynamic-update-slice(f32[4,256,12,64]{1,0,3,2:T(4,128)} %get-tuple-element.1949, f32[1,256,12,64]{1,0,3,2:T(1,128)S(1)} %copy.251, s32[]{:T(128)S(6)} %sub.193, s32[]{:T(128)} %constant.172.clone.1..sunk, s32[]{:T(128)} %constant.172.clone.1..sunk, s32[]{:T(128)} %constant.172.clone.1..sunk) | dynamic-update-slice | bytes 1572868 | tf_op jit(solution)/shard_map/transpose(jvp())/while/body/jit(dynamic_update_index_in_dim)/dynamic_update_slice | solution.py:59
  454.4 6.8 fusion.239
  478.2 17.9 %dynamic_update_slice.208 = f32[4,256,12,64]{1,0,3,2:T(4,128)} dynamic-update-slice(f32[4,256,12,64]{1,0,3,2:T(4,128)} %get-tuple-element.1949, f32[1,256,12,64]{1,0,3,2:T(1,128)S(1)} %copy.251, s32[]{:T(128)S(6)} %sub.193, s32[]{:T(128)} %constant.172.clone.1..sunk, s32[]{:T(128)} %constant.172.clone.1..sunk, s32[]{:T(128)} %constant.172.clone.1..sunk) | dynamic-update-slice | bytes 1572868 | tf_op jit(solution)/shard_map/transpose(jvp())/while/body/jit(dynamic_update_index_in_dim)/dynamic_update_slice | solution.py:59
  510.4 6.8 fusion.239
  534.2 17.9 %dynamic_update_slice.208 = f32[4,256,12,64]{1,0,3,2:T(4,128)} dynamic-update-slice(f32[4,256,12,64]{1,0,3,2:T(4,128)} %get-tuple-element.1949, f32[1,256,12,64]{1,0,3,2:T(1,128)S(1)} %copy.251, s32[]{:T(128)S(6)} %sub.193, s32[]{:T(128)} %constant.172.clone.1..sunk, s32[]{:T(128)} %constant.172.clone.1..sunk, s32[]{:T(128)} %constant.172.clone.1..sunk) | dynamic-update-slice | bytes 1572868 | tf_op jit(solution)/shard_map/transpose(jvp())/while/body/jit(dynamic_update_index_in_dim)/dynamic_update_slice | solution.py:59
  579.3 6.5 broadcast_multiply_fusion
  588.1 8.2 pad_add_fusion
  604.9 26.2 %all-reduce.14 = bf16[1024,256]{1,0:T(8,128)(2,1)} all-reduce(f32[1024,256]{1,0:T(8,128)S(1)} %pad_add_fusion.1), channel_id=1, replica_groups=mesh['dp'=16,'tensor'=2] {'tensor'}, use_global_device_ids=true, to_apply=%region_22.23 | all-reduce | flops 262144 | bytes 1572864 | tf_op jit(solution)/shard_map/psum | solution.py:148
  656.8 30.5 %reduce-scatter.11.cloned.1.call-done = f32[512,768]{1,0:T(8,128)} async-done(((f32[1024,768]{1,0:T(8,128)}), f32[512,768]{1,0:T(8,128)}) %reduce-scatter.11.cloned.1.call-update) | async-done | bytes 1572880 | tf_op jit(solution)/shard_map/reduce_scatter | solution.py:157
  690.1 57.8 %reduce-scatter.17.cloned.1.call-done = f32[2,48,128]{2,1,0:T(8,128)} async-done(((f32[2,768,128]{2,1,0:T(8,128)}), f32[2,48,128]{2,1,0:T(8,128)}) %reduce-scatter.17.cloned.1.call-update) | async-done | bytes 49168 | tf_op jit(solution)/shard_map/reduce_scatter | solution.py:206
  748.0 10.1 %all-reduce.12 = (f32[768]{0:T(1024)S(1)}, f32[2,4,128]{2,1,0:T(4,128)S(1)}, f32[2,128]{1,0:T(2,128)S(1)}, f32[2,48,128]{2,1,0:T(8,128)}) all-reduce(f32[768]{0:T(1024)} %get-tuple-element.1290, f32[2,4,128]{2,1,0:T(4,128)} %pad_maximum_fusion.5, f32[2,128]{1,0:T(2,128)} %pad_maximum_fusion.6, ...), channel_id=1, replica_groups=mesh['dp'=16,'tensor'=2] {'tensor'}, use_global_device_ids=true, to_apply=%region_25.26 | all-reduce | flops 14336 | bytes 114688 | tf_op jit(solution)/shard_map/psum | solution.py:201
  758.1 58.8 %all-reduce.11 = (f32[768]{0:T(1024)}, f32[4,768]{1,0:T(4,128)}, f32[768]{0:T(1024)}, f32[2,4,128]{2,1,0:T(4,128)}, f32[2,128]{1,0:T(2,128)}, /*index=5*/f32[12]...) all-reduce(f32[768]{0:T(1024)S(1)} %get-tuple-element.1405, ...), channel_id=1, replica_groups=mesh['dp'=16,'tensor'=2] {'dp'}, use_global_device_ids=true, to_apply=%region_26.27 | all-reduce | flops 6692 | bytes 53536 | tf_op jit(solution)/shard_map/psum | solution.py:208
  820.7 39.3 %reduce-scatter.15.cloned.1.call-done = f32[768,48]{0,1:T(8,128)} async-done(((f32[768,768]{0,1:T(8,128)}), f32[768,48]{0,1:T(8,128)}) %reduce-scatter.15.cloned.1.call-update) | async-done | bytes 147472 | tf_op jit(solution)/shard_map/reduce_scatter | solution.py:205
  860.0 79.4 %reduce-scatter.13.cloned.1.call-done = f32[2,48,768]{2,1,0:T(8,128)} async-done(((f32[2,768,768]{2,1,0:T(8,128)}), f32[2,48,768]{2,1,0:T(8,128)}) %reduce-scatter.13.cloned.1.call-update) | async-done | bytes 294928 | tf_op jit(solution)/shard_map/reduce_scatter | solution.py:203
  (516 shorter events, 325.9 us)
Async XLA Ops:
  7.2 31.5 %copy-start.66 = (f32[2,128]{1,0:T(2,128)S(1)}, f32[2,128]{1,0:T(2,128)}, u32[]{:S(2)}) copy-start(f32[2,128]{1,0:T(2,128)} %param.28) | copy-start | bytes 3076
  7.2 31.6 %copy-start.61 = (bf16[48,12]{0,1:T(8,128)(2,1)S(1)}, bf16[48,12]{0,1:T(8,128)(2,1)}, u32[]{:S(2)}) copy-start(bf16[48,12]{0,1:T(8,128)(2,1)} %param.23) | copy-start | bytes 3460
  7.2 49.4 %copy-start.70 = (f32[12]{0:T(128)S(1)}, f32[12]{0:T(128)}, u32[]{:S(2)}) copy-start(f32[12]{0:T(128)} %param.30) | copy-start | bytes 148
  7.2 49.4 %copy-start.69 = (f32[12]{0:T(128)S(1)}, f32[12]{0:T(128)}, u32[]{:S(2)}) copy-start(f32[12]{0:T(128)} %param.31) | copy-start | bytes 148
  7.3 49.6 %copy-start.63 = (f32[768]{0:T(1024)S(1)}, f32[768]{0:T(1024)}, u32[]{:S(2)}) copy-start(f32[768]{0:T(1024)} %param.26) | copy-start | bytes 9220
  7.3 49.6 %copy-start.67 = (f32[12]{0:T(128)S(1)}, f32[12]{0:T(128)}, u32[]{:S(2)}) copy-start(f32[12]{0:T(128)} %param.29) | copy-start | bytes 148
  7.3 49.6 %all-gather.6.cloned.1.call-start = ((), (), s32[]{:S(2)}) async-start(), calls=%async_computation.6 | async-start | bytes 2359296 | tf_op jit(solution)/shard_map/all_gather | solution.py:103
  12.1 74.6 %all-gather.8.cloned.1.call-start = ((), (), s32[]{:S(2)}) async-start(), calls=%async_computation.7 | async-start | bytes 2506752 | tf_op jit(solution)/shard_map/all_gather | solution.py:91
  12.9 293.6 %all-gather.12.cloned.1.call-start = ((), (), s32[]{:S(2)}) async-start(), calls=%async_computation.10 | async-start | bytes 2359296 | tf_op jit(solution)/shard_map/all_gather | solution.py:128
  13.6 292.8 %all-gather.10.cloned.1.call-start = ((), (), s32[]{:S(2)}) async-start(), calls=%async_computation.8 | async-start | bytes 1253376 | tf_op jit(solution)/shard_map/all_gather | solution.py:94
  14.2 641.2 %reduce-scatter.19.cloned.1.call-start = ((), (), s32[]{:S(2)}) async-start(), calls=%async_computation.15 | async-start | bytes 417792
  38.6 51.3 %copy-start.27 = (bf16[768,128]{1,0:T(8,128)(2,1)}, bf16[768,128]{1,0:T(8,128)(2,1)S(1)}, u32[]{:S(2)}) copy-start(bf16[768,128]{1,0:T(8,128)(2,1)S(1)} %get-tuple-element.1446) | copy-start | bytes 589828
  38.7 51.3 %copy-start.29 = (bf16[768,128]{1,0:T(8,128)(2,1)}, bf16[768,128]{1,0:T(8,128)(2,1)S(1)}, u32[]{:S(2)}) copy-start(bf16[768,128]{1,0:T(8,128)(2,1)S(1)} %get-tuple-element.1447) | copy-start | bytes 589828
  38.7 51.2 %copy-start.38 = (f32[1,1024]{1,0:T(1,128)}, f32[1,1024]{1,0:T(1,128)S(1)}, u32[]{:S(2)}) copy-start(f32[1,1024]{1,0:T(1,128)S(1)} %get-tuple-element.1453) | copy-start | bytes 12292
  38.7 51.2 %copy-start.40 = (f32[1,1024]{1,0:T(1,128)}, f32[1,1024]{1,0:T(1,128)S(1)}, u32[]{:S(2)}) copy-start(f32[1,1024]{1,0:T(1,128)S(1)} %get-tuple-element.1454) | copy-start | bytes 12292
  38.8 51.2 %copy-start.42 = (f32[1,1024]{1,0:T(1,128)}, f32[1,1024]{1,0:T(1,128)S(1)}, u32[]{:S(2)}) copy-start(f32[1,1024]{1,0:T(1,128)S(1)} %get-tuple-element.1455) | copy-start | bytes 12292
  38.8 51.2 %copy-start.44 = (f32[1,1024]{1,0:T(1,128)}, f32[1,1024]{1,0:T(1,128)S(1)}, u32[]{:S(2)}) copy-start(f32[1,1024]{1,0:T(1,128)S(1)} %get-tuple-element.1456) | copy-start | bytes 12292
  56.7 33.3 %copy-start.34 = (bf16[768,12]{0,1:T(8,128)(2,1)}, bf16[768,12]{0,1:T(8,128)(2,1)S(1)}, u32[]{:S(2)}) copy-start(bf16[768,12]{0,1:T(8,128)(2,1)S(1)} %reshape.337) | copy-start | bytes 55300
  56.8 260.9 %copy-start.47 = (f32[768]{0:T(1024)}, f32[768]{0:T(1024)S(1)}, u32[]{:S(2)}) copy-start(f32[768]{0:T(1024)S(1)} %mul.593) | copy-start | bytes 9220
  579.2 71.8 %copy-start.51 = (f32[1024]{0:T(1024)}, f32[1024]{0:T(1024)S(1)}, u32[]{:S(2)}) copy-start(f32[1024]{0:T(1024)S(1)} %get-tuple-element.1283) | copy-start | bytes 12292
  579.2 71.8 %copy-start.52 = (f32[1024]{0:T(1024)}, f32[1024]{0:T(1024)S(1)}, u32[]{:S(2)}) copy-start(f32[1024]{0:T(1024)S(1)} %get-tuple-element.1284) | copy-start | bytes 12292
  579.2 71.8 %copy-start.53 = (f32[1024]{0:T(1024)}, f32[1024]{0:T(1024)S(1)}, u32[]{:S(2)}) copy-start(f32[1024]{0:T(1024)S(1)} %get-tuple-element.1285) | copy-start | bytes 12292
  588.0 99.3 %reduce-scatter.11.cloned.1.call-start = ((), (), s32[]{:S(2)}) async-start(), calls=%async_computation.11 | async-start | bytes 4718592 | tf_op jit(solution)/shard_map/reduce_scatter | solution.py:157
  602.3 145.7 %reduce-scatter.17.cloned.1.call-start = ((), (), s32[]{:S(2)}) async-start(), calls=%async_computation.14 | async-start | bytes 835584 | tf_op jit(solution)/shard_map/reduce_scatter | solution.py:206
  633.8 183.8 %reduce-scatter.9.cloned.1.call-start = ((), (), s32[]{:S(2)}) async-start(), calls=%async_computation.9 | async-start | bytes 4718592 | tf_op jit(solution)/shard_map/reduce_scatter | solution.py:121
  638.4 221.5 %reduce-scatter.15.cloned.1.call-start = ((), (), s32[]{:S(2)}) async-start(), calls=%async_computation.13 | async-start | bytes 2506752 | tf_op jit(solution)/shard_map/reduce_scatter | solution.py:205
  643.0 296.4 %reduce-scatter.13.cloned.1.call-start = ((), (), s32[]{:S(2)}) async-start(), calls=%async_computation.12 | async-start | bytes 5013504 | tf_op jit(solution)/shard_map/reduce_scatter | solution.py:203
  650.8 36.5 %copy-start.12 = (bf16[512,768]{1,0:T(8,128)(2,1)S(1)}, bf16[512,768]{1,0:T(8,128)(2,1)}, u32[]{:S(2)}) copy-start(bf16[512,768]{1,0:T(8,128)(2,1)} %param.19) | copy-start | bytes 2359300
  650.8 36.5 %copy-start.28 = (bf16[768,128]{1,0:T(8,128)(2,1)S(1)}, bf16[768,128]{1,0:T(8,128)(2,1)}, u32[]{:S(2)}) copy-start(bf16[768,128]{1,0:T(8,128)(2,1)} %copy-done.27) | copy-start | bytes 589828
  650.9 36.5 %copy-start.30 = (bf16[768,128]{1,0:T(8,128)(2,1)S(1)}, bf16[768,128]{1,0:T(8,128)(2,1)}, u32[]{:S(2)}) copy-start(bf16[768,128]{1,0:T(8,128)(2,1)} %copy-done.29) | copy-start | bytes 589828
  650.9 36.4 %copy-start.46 = (f32[768]{0:T(1024)S(1)}, f32[768]{0:T(1024)}, u32[]{:S(2)}) copy-start(f32[768]{0:T(1024)} %param.21) | copy-start | bytes 9220
  650.9 166.7 %copy-start.16 = (bf16[512,768]{1,0:T(8,128)(2,1)S(1)}, bf16[512,768]{1,0:T(8,128)(2,1)}, u32[]{:S(2)}) copy-start(bf16[512,768]{1,0:T(8,128)(2,1)} %param.20) | copy-start | bytes 2359300
  (50 other events, 296.6 us)
Sparse Core Ops, SparseCore 0:
  12.2 29.8 all-gather.5
  44.5 42.2 all-gather.7
  88.3 25.9 all-gather.11
  116.5 38.3 all-gather.9
  588.1 54.4 reduce-scatter.18
  644.9 42.3 reduce-scatter.10
  691.4 56.5 reduce-scatter.16
  750.3 42.4 reduce-scatter.8
  797.1 62.8 reduce-scatter.14
  864.7 74.5 reduce-scatter.12
where the time goes:
time: 950 us; the launch traced here: 946 us
  local copies, waits for them, and re-layouts  263 us (28%)
  waiting for transfers between devices  236 us (25%)
  matrix products  166 us (17%)
  blocking collectives  148 us (16%)
  other arithmetic  116 us (12%)
  between operations  15.4 us (2%)
    dynamic_update_slice x52, local copies, waits for them, and re-layouts, ssd_local(): lax.scan(ssd_block, initial, (by_block(heads_in), by_block(inject), by_bl...  172 us
    reduce_scatter x1, waiting for transfers between devices, body(): lax.psum_scatter(grad_w_zx, 'dp', scatter_dimension=1, tiled=True)  79.4 us
    dot_general x12, matrix products, ssd_block(): within = jnp.einsum('ijh,jhp->ihp', mixing, signal, precision=HIGH)  62.7 us
    psum x1, blocking collectives, body(): lax.psum((grad_kernel[:, :channels], grad_kernel_bias[:channels], grad_dt...  58.8 us
    reduce_scatter x1, waiting for transfers between devices, body(): lax.psum_scatter(shared[0], 'dp', scatter_dimension=1, tiled=True)  57.8 us
    reduce_scatter x1, waiting for transfers between devices, body(): lax.psum_scatter(grad_w_out, 'dp', scatter_dimension=1, tiled=True)  39.3 us
    dynamic_update_slice x16, other arithmetic, ssd_local(): lax.scan(ssd_block, initial, (by_block(heads_in), by_block(inject), by_bl...  30.6 us
    reduce_scatter x1, waiting for transfers between devices, body(): lax.psum_scatter(summed + lax.dot_general(d_dt_low, full_dt, CONTRACT_LAS...  30.5 us
  transfers between devices with their start and end apart: 10, of which 5 were waited for; matrix products, arithmetic and copies ran while one was open for 28% of the time, Pallas kernels for 0%

commit v1 on v0

v1 whole, which is shorter than its diff:
```python
import functools

import jax
import jax.numpy as jnp
from jax import lax
from jax.experimental import pallas as pl
from jax.experimental.pallas import tpu as pltpu
from jax.sharding import PartitionSpec as P

Q = 256
EPS = 1e-05
HIGH = lax.Precision.HIGHEST
F32 = jnp.float32
BF16 = jnp.bfloat16
NN = (((1,), (0,)), ((), ()))
NT = (((1,), (1,)), ((), ()))
TN = (((0,), (0,)), ((), ()))
LANES = 128
DT_AT = 16


def dot(a, b, dims=NN):
    return lax.dot_general(a, b, dims, preferred_element_type=F32)


def rows_of(ref, first, count, columns):
    return ref[pl.ds(first, count), columns]


def scan_forward(heads, taps, xp_ref, col_ref, row_ref, w_ref, skip_ref, mixed_ref, pre_ref, states_ref, buf, act, st):
    channels = skip_ref.shape[1]
    wide = xp_ref.shape[1]
    state_size = (wide - channels) // 2

    @pl.when(pl.program_id(0) == 0)
    def _():
        st[...] = jnp.zeros_like(st)
        buf[0:8, :] = jnp.zeros((8, wide), F32)

    buf[8 : 8 + Q, :] = xp_ref[...]
    for start in range(0, wide, LANES):
        cols = pl.ds(start, LANES)
        pre = w_ref[taps : taps + 1, cols] + jnp.zeros((Q, LANES), F32)
        for k in range(taps):
            pre = pre + w_ref[k : k + 1, cols] * buf[9 - taps + k : 9 - taps + k + Q, cols]
        pre_ref[:, cols] = pre
        act[:, cols] = (pre * jax.nn.sigmoid(pre)).astype(BF16)
    buf[0:8, :] = buf[Q : Q + 8, :]

    inject = act[:, channels : channels + state_size]
    readout = act[:, channels + state_size :]
    affinity = dot(readout, inject, NT)
    mask = lax.broadcasted_iota(jnp.int32, (Q, Q), 0) >= lax.broadcasted_iota(jnp.int32, (Q, Q), 1)
    first = lax.broadcasted_iota(jnp.int32, (1, LANES), 1) < LANES // 2
    states_ref[0] = st[...].astype(BF16)
    for pair in range(heads // 2):
        cols = pl.ds(pair * LANES, LANES)
        signal = act[:, cols]
        parts = []
        for side in range(2):
            h = 2 * pair + side
            gap = col_ref[:, h : h + 1] - row_ref[h : h + 1, :]
            weights = jnp.where(mask, jnp.exp(gap), 0.0)
            mixing = (affinity * weights * row_ref[DT_AT + h : DT_AT + h + 1, :]).astype(BF16)
            parts.append(dot(mixing, signal))
        within = jnp.where(first, parts[0], parts[1])
        run = jnp.where(first, col_ref[:, 2 * pair : 2 * pair + 1], col_ref[:, 2 * pair + 1 : 2 * pair + 2])
        step = jnp.where(
            first,
            col_ref[:, DT_AT + 2 * pair : DT_AT + 2 * pair + 1],
            col_ref[:, DT_AT + 2 * pair + 1 : DT_AT + 2 * pair + 2],
        )
        end = run[Q - 1 : Q, :]
        before = st[:, cols]
        across = jnp.exp(run) * dot(readout, before.astype(BF16))
        wide_signal = signal.astype(F32)
        mixed_ref[:, cols] = within + across + skip_ref[:, cols] * wide_signal
        weighted = (jnp.exp(end - run) * step * wide_signal).astype(BF16)
        st[:, cols] = jnp.exp(end) * before + dot(inject, weighted, TN)


def scan_backward(
    heads, taps, xp_ref, pre_ref, col_ref, row_ref, w_ref, skip_ref, states_ref, dy_ref,
    dx_ref, dbc_ref, colout_ref, rowout_ref, sums_ref, gw_ref, buf, dst, dgs,
):
    channels = skip_ref.shape[1]
    wide = xp_ref.shape[1]
    state_size = (wide - channels) // 2

    @pl.when(pl.program_id(0) == 0)
    def _():
        dst[...] = jnp.zeros_like(dst)
        buf[Q : Q + 8, :] = jnp.zeros((8, wide), F32)
        gw_ref[...] = jnp.zeros_like(gw_ref)

    def act_of(start):
        pre = pre_ref[:, pl.ds(start, LANES)]
        return (pre * jax.nn.sigmoid(pre)).astype(BF16)

    def conv_back(start, d_act):
        cols = pl.ds(start, LANES)
        pre = pre_ref[:, cols]
        s = jax.nn.sigmoid(pre)
        d_pre = d_act * s * (1.0 + pre * (1.0 - s))
        buf[0:Q, cols] = d_pre
        own = xp_ref[:, cols]
        total = jnp.zeros((Q, LANES), F32)
        for k in range(taps):
            moved = buf[taps - 1 - k : taps - 1 - k + Q, cols]
            total = total + w_ref[k : k + 1, cols] * moved
            gw_ref[k : k + 1, cols] += jnp.sum(own * moved, axis=0, keepdims=True)
        gw_ref[taps : taps + 1, cols] += jnp.sum(d_pre, axis=0, keepdims=True)
        buf[Q : Q + 8, cols] = d_pre[0:8, :]
        return total.astype(BF16)

    inject = act_of(channels)
    readout = act_of(channels + state_size)
    affinity = dot(readout, inject, NT)
    mask = lax.broadcasted_iota(jnp.int32, (Q, Q), 0) >= lax.broadcasted_iota(jnp.int32, (Q, Q), 1)
    lane = lax.broadcasted_iota(jnp.int32, (1, LANES), 1)
    first = lane < LANES // 2
    d_inject = jnp.zeros((Q, state_size), F32)
    d_readout = jnp.zeros((Q, state_size), F32)
    colout = jnp.zeros((Q, LANES), F32)
    dgs[...] = jnp.zeros_like(dgs)
    for pair in range(heads // 2):
        cols = pl.ds(pair * LANES, LANES)
        signal = act_of(pair * LANES)
        wide_signal = signal.astype(F32)
        d_low = dy_ref[:, cols]
        d_wide = d_low.astype(F32)
        before = states_ref[0, :, cols]
        d_after = dst[:, cols]
        d_after_low = d_after.astype(BF16)
        run = jnp.where(first, col_ref[:, 2 * pair : 2 * pair + 1], col_ref[:, 2 * pair + 1 : 2 * pair + 2])
        step = jnp.where(
            first,
            col_ref[:, DT_AT + 2 * pair : DT_AT + 2 * pair + 1],
            col_ref[:, DT_AT + 2 * pair + 1 : DT_AT + 2 * pair + 2],
        )
        end = run[Q - 1 : Q, :]
        grown = jnp.exp(run)
        to_end = jnp.exp(end - run)
        d_across = (grown * d_wide).astype(BF16)
        across_part = grown * d_wide * dot(readout, before)
        from_state = dot(inject, d_after_low)
        end_part = wide_signal * from_state
        d_readout += dot(d_across, before, NT)
        d_inject += dot((to_end * step * wide_signal).astype(BF16), d_after_low, NT)
        parts = []
        for side in range(2):
            h = 2 * pair + side
            mine = first if side == 0 else ~first
            gap = col_ref[:, h : h + 1] - row_ref[h : h + 1, :]
            weights = jnp.where(mask, jnp.exp(gap), 0.0)
            stepped = weights * row_ref[DT_AT + h : DT_AT + h + 1, :]
            plain = affinity * weights
            d_mixing = dot(d_low, jnp.where(mine, signal, jnp.zeros_like(signal)), NT)
            dgs[...] += d_mixing * stepped
            pulled = d_mixing * plain
            rowout_ref[h : h + 1, :] = jnp.sum(pulled, axis=0, keepdims=True)
            along = jnp.sum(pulled * row_ref[DT_AT + h : DT_AT + h + 1, :], axis=1, keepdims=True)
            along = along + jnp.sum(jnp.where(mine, across_part, 0.0), axis=1, keepdims=True)
            ended = jnp.sum(jnp.where(mine, end_part, 0.0), axis=1, keepdims=True)
            colout = jnp.where(lane == h, along, colout)
            colout = jnp.where(lane == DT_AT + h, ended, colout)
            parts.append(dot(plain.astype(BF16), d_low, TN))
        within = jnp.where(first, parts[0], parts[1])
        d_signal = step * (within + to_end * from_state) + skip_ref[:, cols] * d_wide
        grown_end = jnp.exp(end)
        sums_ref[0, 0:1, cols] = grown_end * jnp.sum(d_after * before.astype(F32), axis=0, keepdims=True)
        sums_ref[0, 1:2, cols] = jnp.sum(d_wide * wide_signal, axis=0, keepdims=True)
        dst[:, cols] = grown_end * d_after + dot(readout, d_across, TN)
        dx_ref[:, cols] = conv_back(pair * LANES, d_signal)
    colout_ref[...] = colout
    d_affinity = dgs[...].astype(BF16)
    d_readout += dot(d_affinity, inject)
    d_inject += dot(d_affinity, readout, TN)
    dbc_ref[:, :state_size] = conv_back(channels, d_inject)
    dbc_ref[:, state_size:] = conv_back(channels + state_size, d_readout)


def whole_block(shape):
    return pl.BlockSpec(shape, lambda i: (0,) * len(shape))


def run_forward(xp, col, row, w, skip, heads, taps):
    length, wide = xp.shape[0], w.shape[1]
    channels = skip.shape[1]
    chunks = length // Q
    state_size = (wide - channels) // 2
    return pl.pallas_call(
        functools.partial(scan_forward, heads, taps),
        grid=(chunks,),
        in_specs=[
            pl.BlockSpec((Q, wide), lambda i: (i, 0)),
            pl.BlockSpec((Q, LANES), lambda i: (i, 0)),
            pl.BlockSpec((2 * DT_AT, Q), lambda i: (0, i)),
            whole_block(w.shape),
            whole_block(skip.shape),
        ],
        out_specs=[
            pl.BlockSpec((Q, channels), lambda i: (i, 0)),
            pl.BlockSpec((Q, wide), lambda i: (i, 0)),
            pl.BlockSpec((1, state_size, channels), lambda i: (i, 0, 0)),
        ],
        out_shape=[
            jax.ShapeDtypeStruct((length, channels), F32),
            jax.ShapeDtypeStruct((length, wide), F32),
            jax.ShapeDtypeStruct((chunks, state_size, channels), BF16),
        ],
        scratch_shapes=[
            pltpu.VMEM((Q + 8, wide), F32),
            pltpu.VMEM((Q, wide), BF16),
            pltpu.VMEM((state_size, channels), F32),
        ],
        compiler_params=pltpu.CompilerParams(vmem_limit_bytes=40 * 2**20),
        cost_estimate=pl.CostEstimate(flops=20 * 10**9, bytes_accessed=13 * 10**6, transcendentals=5 * 10**6),
        name="scan_forward",
    )(xp, col, row, w, skip)


def run_backward(xp, pre, col, row, w, skip, states, dy, heads, taps):
    length, wide = pre.shape
    channels = skip.shape[1]
    chunks = length // Q
    state_size = (wide - channels) // 2
    back = lambda i: (chunks - 1 - i, 0)
    return pl.pallas_call(
        functools.partial(scan_backward, heads, taps),
        grid=(chunks,),
        in_specs=[
            pl.BlockSpec((Q, wide), back),
            pl.BlockSpec((Q, wide), back),
            pl.BlockSpec((Q, LANES), back),
            pl.BlockSpec((2 * DT_AT, Q), lambda i: (0, chunks - 1 - i)),
            whole_block(w.shape),
            whole_block(skip.shape),
            pl.BlockSpec((1, state_size, channels), lambda i: (chunks - 1 - i, 0, 0)),
            pl.BlockSpec((Q, channels), back),
        ],
        out_specs=[
            pl.BlockSpec((Q, channels), back),
            pl.BlockSpec((Q, 2 * state_size), back),
            pl.BlockSpec((Q, LANES), back),
            pl.BlockSpec((DT_AT, Q), lambda i: (0, chunks - 1 - i)),
            pl.BlockSpec((1, 2, channels), lambda i: (chunks - 1 - i, 0, 0)),
            whole_block(w.shape),
        ],
        out_shape=[
            jax.ShapeDtypeStruct((length, channels), BF16),
            jax.ShapeDtypeStruct((length, 2 * state_size), BF16),
            jax.ShapeDtypeStruct((length, LANES), F32),
            jax.ShapeDtypeStruct((DT_AT, length), F32),
            jax.ShapeDtypeStruct((chunks, 2, channels), F32),
            jax.ShapeDtypeStruct(w.shape, F32),
        ],
        scratch_shapes=[
            pltpu.VMEM((Q + 8, wide), F32),
            pltpu.VMEM((state_size, channels), F32),
            pltpu.VMEM((Q, Q), F32),
        ],
        compiler_params=pltpu.CompilerParams(vmem_limit_bytes=40 * 2**20),
        cost_estimate=pl.CostEstimate(flops=40 * 10**9, bytes_accessed=15 * 10**6, transcendentals=5 * 10**6),
        name="scan_backward",
    )(xp, pre, col, row, w, skip, states, dy)


def swap(x, axis, bit):
    size = lax.axis_size(axis)
    return lax.ppermute(x, axis, [(i, i ^ bit) for i in range(size)])


def bits_of(axis):
    size = lax.axis_size(axis)
    return [1 << k for k in range(size.bit_length() - 1)]


def my_bit(axis, bit):
    return (lax.axis_index(axis) // bit) % 2


def both(own, other, second):
    return jnp.where(second == 1, jnp.stack([other, own]), jnp.stack([own, other]))


def gather_rows(block):
    bits = bits_of("dp")
    order = [b for b in bits if b > 2] + [b for b in bits if b == 2] + [b for b in bits if b == 1]
    x = block
    for bit in order:
        x = both(x, swap(x, "dp", bit), my_bit("dp", bit))
    done = order[::-1]
    axes = [done.index(b) for b in bits[::-1]]
    count = len(bits)
    x = jnp.transpose(x, axes + list(range(count, count + block.ndim)))
    return x.reshape((-1,) + block.shape[1:])


def scatter_rows(x):
    bits = bits_of("dp")
    left = bits[::-1]
    x = x.reshape((2,) * len(bits) + (x.shape[0] >> len(bits), x.shape[1]))
    for bit in bits:
        axis = left.index(bit)
        mine = my_bit("dp", bit)
        keep = lax.dynamic_index_in_dim(x, mine, axis, keepdims=False)
        send = lax.dynamic_index_in_dim(x, 1 - mine, axis, keepdims=False).astype(BF16)
        x = keep.astype(F32) + swap(send, "dp", bit).astype(F32)
        left.remove(bit)
    return x


def sum_dp(x):
    for bit in bits_of("dp"):
        x = x + swap(x, "dp", bit)
    return x


def body(
    residual, grad_out, norm_gain, w_zx, w_dt, w_bc, conv_x, conv_x_bias, conv_bc, conv_bc_bias,
    dt_bias, a_log, d_skip, gate_gain, w_out,
):
    own_rows, width = residual.shape
    channels = gate_gain.shape[0]
    all_channels = channels * lax.axis_size("tensor")
    state_size = w_bc.shape[2]
    heads = dt_bias.shape[0]
    head_size = channels // heads
    taps = conv_x.shape[0]
    wide = channels + 2 * state_size
    side = lax.axis_index("tensor")

    def own_half(x):
        return lax.dynamic_slice_in_dim(x, side * own_rows, own_rows, 0)

    def other_half(x):
        return lax.dynamic_slice_in_dim(x, (1 - side) * own_rows, own_rows, 0)

    pad_dt = LANES - heads
    weights_in = gather_rows(
        jnp.concatenate([w_zx[1], w_bc[0], w_bc[1], jnp.pad(w_dt, ((0, 0), (0, pad_dt)))], axis=1)
    )
    weights_side = gather_rows(jnp.concatenate([w_zx[0], w_out.T], axis=1))
    weight_gate, weight_out_t = weights_side[:, :channels], weights_side[:, channels:]

    rows = both(residual, swap(residual, "tensor", 1), side).reshape(2 * own_rows, width).astype(F32)
    cotangent = both(grad_out, swap(grad_out, "tensor", 1), side).reshape(2 * own_rows, width)
    in_scale = lax.rsqrt(jnp.mean(rows * rows, axis=1, keepdims=True) + EPS)
    normed = (rows * in_scale * norm_gain).astype(BF16)

    projected = dot(normed, weights_in)
    dt_in = projected[:, wide : wide + heads] + dt_bias
    timestep = jax.nn.softplus(dt_in)
    rate = -jnp.exp(a_log)
    decays = timestep * rate
    length = decays.shape[0]
    chunks = length // Q
    tri = jnp.tril(jnp.ones((Q, Q), F32))
    running = jnp.einsum("ij,cjh->cih", tri, decays.reshape(chunks, Q, heads), precision=HIGH)
    running_flat = running.reshape(length, heads)
    gap = jnp.zeros((length, DT_AT - heads), F32)
    packed = jnp.concatenate([running_flat, gap, timestep, gap], axis=1)
    col = jnp.pad(packed, ((0, 0), (0, LANES - 2 * DT_AT)))
    row = packed.T
    taps_all = jnp.concatenate([conv_x, conv_bc[0], conv_bc[1]], axis=1)
    bias_all = jnp.concatenate([conv_x_bias, conv_bc_bias[0], conv_bc_bias[1]])
    w = jnp.concatenate([taps_all, bias_all[None], jnp.zeros((8 - taps - 1, wide), F32)], axis=0)
    skip = jnp.repeat(d_skip, head_size)[None]
    mixed, pre, states = run_forward(projected, col, row, w, skip, heads, taps)

    gate_pre = dot(normed, weight_gate)
    d_gated = dot(cotangent, weight_out_t)
    logistic = jax.nn.sigmoid(gate_pre)
    gate_act = gate_pre * logistic
    gated_in = mixed * gate_act
    scaled_grad = d_gated * gate_gain
    sums = jnp.stack([jnp.sum(gated_in * gated_in, axis=1), jnp.sum(scaled_grad * gated_in, axis=1)])
    sums = sums + swap(sums, "tensor", 1)
    out_scale = lax.rsqrt(sums[0] / all_channels + EPS)[:, None]
    gated = (gated_in * out_scale * gate_gain).astype(BF16)
    d_inner = out_scale * scaled_grad - gated_in * (out_scale**3 * sums[1][:, None] / all_channels)
    d_mixed = (d_inner * gate_act).astype(BF16)
    d_gate = (d_inner * mixed * logistic * (1.0 + gate_pre * (1.0 - logistic))).astype(BF16)
    grad_gate_gain = jnp.sum(d_gated * gated_in * out_scale, axis=0)

    sent = swap(dot(other_half(gated), weight_out_t, NT).astype(BF16), "tensor", 1)
    branch = dot(own_half(gated), weight_out_t, NT) + sent.astype(F32)
    layer_out = (residual.astype(F32) + branch).astype(BF16)

    grad_side = scatter_rows(
        jnp.concatenate([dot(normed, d_gate, TN), dot(cotangent, gated, TN)], axis=1)
    )
    d_x, d_bc, colout, rowout, chunk_sums, grad_w = run_backward(
        projected, pre, col, row, w, skip, states, d_mixed, heads, taps
    )

    along = colout[:, :heads].reshape(chunks, Q, heads)
    ended = colout[:, DT_AT : DT_AT + heads].reshape(chunks, Q, heads)
    pulled = rowout[:heads].T.reshape(chunks, Q, heads)
    steps = timestep.reshape(chunks, Q, heads)
    d_step = pulled + jnp.exp(running[:, -1:] - running) * ended
    to_end = steps * jnp.exp(running[:, -1:] - running) * ended
    d_running = along - steps * d_step
    per_head = jnp.sum(chunk_sums.reshape(chunks, 2, heads, head_size), axis=3)
    at_end = jnp.sum(to_end, axis=1) + per_head[:, 0]
    d_decays = jnp.einsum("ji,cjh->cih", tri, d_running, precision=HIGH) + at_end[:, None]
    d_decays = d_decays.reshape(length, heads)
    d_dt = (d_step.reshape(length, heads) + d_decays * rate) * jax.nn.sigmoid(dt_in)
    grad_dt_bias = jnp.sum(d_dt, axis=0)
    grad_a_log = jnp.sum(d_decays * decays, axis=0)
    grad_d_skip = jnp.sum(per_head[:, 1], axis=0)

    d_shared = d_bc.astype(F32) + swap(d_bc, "tensor", 1).astype(F32)
    d_shared = d_shared.astype(BF16)
    d_dt_low = jnp.pad(d_dt.astype(BF16), ((0, 0), (0, pad_dt)))
    grad_in = scatter_rows(dot(normed, jnp.concatenate([d_x, d_shared, d_dt_low], axis=1), TN))
    d_all = jnp.concatenate([d_x, d_shared * 0.5, d_dt_low, d_gate], axis=1)
    weights_all = jnp.concatenate([weights_in, weight_gate], axis=1)
    partial = dot(d_all, weights_all, NT)
    received = swap(other_half(partial).astype(BF16), "tensor", 1)
    grad_norm_gain = jnp.sum(partial * rows * in_scale, axis=0)

    shared = jnp.concatenate([grad_norm_gain, grad_w[: taps + 1, channels:].reshape(-1)])
    shared = shared + swap(shared, "tensor", 1)
    heads_part = jnp.concatenate([grad_dt_bias, grad_a_log, grad_d_skip])
    small = jnp.concatenate(
        [grad_gate_gain, grad_w[: taps + 1, :channels].reshape(-1), shared, heads_part]
    )
    count = small.shape[0]
    small = jnp.pad(small, (0, -count % 1024)).reshape(-1, LANES)
    small = sum_dp(small).reshape(-1)
    pieces, at = [], 0
    for size in (channels, (taps + 1) * channels, width, (taps + 1) * 2 * state_size, heads, heads, heads):
        pieces.append(small[at : at + size])
        at += size
    sum_gate_gain, sum_conv, sum_norm, sum_bc, sum_dt_bias, sum_a_log, sum_skip = pieces
    sum_conv = sum_conv.reshape(taps + 1, channels)
    sum_bc = sum_bc.reshape(taps + 1, 2, state_size).transpose(1, 0, 2)

    d_normed = own_half(partial) + received.astype(F32)
    own_scale = own_half(in_scale)
    own = residual.astype(F32)
    weighted = d_normed * norm_gain
    d_residual = (
        grad_out.astype(F32)
        + own_scale * weighted
        - own * own_scale**3 * jnp.mean(weighted * own, axis=1, keepdims=True)
    ).astype(BF16)
    return (
        layer_out,
        d_residual,
        sum_norm,
        jnp.stack([grad_side[:, :channels], grad_in[:, :channels]]),
        grad_in[:, wide : wide + heads],
        jnp.stack([grad_in[:, channels : channels + state_size], grad_in[:, channels + state_size : wide]]),
        sum_conv[:taps],
        sum_conv[taps],
        sum_bc[:, :taps],
        sum_bc[:, taps],
        sum_dt_bias,
        sum_a_log,
        sum_skip,
        sum_gate_gain,
        grad_side[:, channels:].T,
    )


def solution(mesh):
    in_specs = (
        P(("dp", "tensor"), None),
        P(("dp", "tensor"), None),
        P(),
        P(None, "dp", "tensor"),
        P("dp", "tensor"),
        P(None, "dp", None),
        P(None, "tensor"),
        P("tensor"),
        P(),
        P(),
        P("tensor"),
        P("tensor"),
        P("tensor"),
        P("tensor"),
        P("tensor", "dp"),
    )
    out_specs = (
        P(("dp", "tensor"), None),
        P(("dp", "tensor"), None),
        P(),
        P(None, "dp", "tensor"),
        P("dp", "tensor"),
        P(None, "dp", None),
        P(None, "tensor"),
        P("tensor"),
        P(),
        P(),
        P("tensor"),
        P("tensor"),
        P("tensor"),
        P("tensor"),
        P("tensor", "dp"),
    )
    return jax.shard_map(body, mesh=mesh, in_specs=in_specs, out_specs=out_specs, check_vma=False)
```

time: 950 us -> 251 us (0.26)
  local copies, waits for them, and re-layouts: 263 us -> 44.5 us
  waiting for transfers between devices: 236 us -> 55.8 us
  blocking collectives: 148 us -> 0 us
  matrix products: 166 us -> 29.1 us
  other arithmetic: 116 us -> 41.9 us
  Pallas kernels: 0 us -> 39.1 us
  starting transfers between devices: 0.57 us -> 34.8 us
  between operations: 15.4 us -> 1.99 us
    reduce_scatter x5 -> x0, waiting for transfers between devices: 207 us -> none  [the longest x1 79.4 us: body(): lax.psum_scatter(grad_w_zx, 'dp', scatter_dimension=1, tiled=True)]
    dynamic_update_slice x52 -> x0, local copies, waits for them, and re-layouts: 172 us -> none  [ssd_local(): lax.scan(ssd_block, initial, (by_block(heads_in), by_block(inject), by_bl...]
    dot_general x61 -> x11, matrix products: 164 us -> 29.1 us  [the longest x9 27.9 us: dot(): return lax.dot_general(a, b, dims, preferred_element_type=F32)]
    psum x5 -> x0, blocking collectives: 106 us -> none  [the longest x1 58.8 us: body(): lax.psum((grad_kernel[:, :channels], grad_kernel_bias[:channels], grad_dt...]
    ppermute x0 -> x27, waiting for transfers between devices: none -> 55.8 us  [swap(): return lax.ppermute(x, axis, [(i, i ^ bit) for i in range(size)])]
    all_gather x2 -> x0, blocking collectives: 41.9 us -> none  [the longest x1 24.2 us: body(): lax.all_gather(w_bc, 'dp', axis=1, tiled=True)]
    pallas_call x0 -> x2, Pallas kernels: none -> 39.1 us  [the longest x1 27.5 us: run_backward(): pl.pallas_call(functools.partial(scan_backward, heads, taps), grid=(chunk...]
    ppermute x0 -> x27, starting transfers between devices: none -> 34.8 us  [swap(): return lax.ppermute(x, axis, [(i, i ^ bit) for i in range(size)])]
  transfers between devices with their start and end apart: 10 -> 27, of which waited for: 5 -> 11; matrix products, arithmetic and copies ran while one was open for 28% -> 32% of each run, Pallas kernels for 0% -> 5%
where the time goes in v1:
time: 251 us; the launch traced here: 247 us
  waiting for transfers between devices  55.8 us (22%)
  local copies, waits for them, and re-layouts  44.5 us (18%)
  other arithmetic  41.9 us (17%)
  Pallas kernels  39.1 us (16%)
  starting transfers between devices  34.8 us (14%)
  matrix products  29.1 us (12%)
    ppermute x27, waiting for transfers between devices, swap(): return lax.ppermute(x, axis, [(i, i ^ bit) for i in range(size)])  55.8 us
    ppermute x27, starting transfers between devices, swap(): return lax.ppermute(x, axis, [(i, i ^ bit) for i in range(size)])  34.8 us
    dot_general x9, matrix products, dot(): return lax.dot_general(a, b, dims, preferred_element_type=F32)  27.9 us
    pallas_call x1, Pallas kernels, run_backward(): pl.pallas_call(functools.partial(scan_backward, heads, taps), grid=(chunk...  27.5 us
    select_n x15, other arithmetic, both(): jnp.where(second == 1, jnp.stack([other, own]), jnp.stack([own, other]))  12.5 us
    pallas_call x1, Pallas kernels, run_forward(): pl.pallas_call(functools.partial(scan_forward, heads, taps), grid=(chunks...  11.6 us
    unnamed x91, local copies, waits for them, and re-layouts  11 us
    convert_element_type x1, other arithmetic, body(): d_mixed = (d_inner * gate_act).astype(BF16)  6.57 us
  transfers between devices with their start and end apart: 27, of which 11 were waited for; matrix products, arithmetic and copies ran while one was open for 32% of the time, Pallas kernels for 5%

profile of v1, /device:TPU:0, one launch (start us, length us, event | category | flops | bytes accessed | tf_op | source)
XLA Modules:
  0.0 247.2 jit_solution(262712170436114506)
XLA Ops:
  3.1 3.1 %collective-permute-start.1 = (bf16[48,1152]{1,0:T(8,128)(2,1)S(1)}, bf16[48,1152]{1,0:T(8,128)(2,1)S(1)}, u32[]{:S(2)}, u32[]{:S(2)}) collective-permute-start(bf16[48,1152]{1,0:T(8,128)(2,1)S(1)} %fusion.59), channel_id=1, source_target_pairs={{0,8},{2,10},{4,12},{6,14},{8,0},{10,2},{12,4},{14,6},{16,24},{18,... | collective-permute-start | bytes 331784 | tf_op jit(solution)/shard_map/ppermute | solution.py:271
  13.2 3.0 %collective-permute-start.2 = (bf16[2,48,1152]{2,1,0:T(8,128)(2,1)S(1)}, bf16[2,48,1152]{2,1,0:T(8,128)(2,1)S(1)}, u32[]{:S(2)}, u32[]{:S(2)}) collective-permute-start(bf16[2,48,1152]{2,1,0:T(8,128)(2,1)S(1)} %maximum_select_fusion.14), channel_id=1, source_target_pairs={{0,16},{2,18},{4,20},{6,22},{8,24},{10,26},{12,28},{14,30},{16,0},... | collective-permute-start | bytes 663560 | tf_op jit(solution)/shard_map/ppermute | solution.py:271
  16.6 16.2 %collective-permute-done.2 = bf16[2,48,1152]{2,1,0:T(8,128)(2,1)S(1)} collective-permute-done((bf16[2,48,1152]{2,1,0:T(8,128)(2,1)S(1)}, bf16[2,48,1152]{2,1,0:T(8,128)(2,1)S(1)}, u32[]{:S(2)}, u32[]{:S(2)}) %collective-permute-start.2) | collective-permute-done | bytes 221216 | tf_op jit(solution)/shard_map/ppermute | solution.py:271
  34.7 3.3 %collective-permute-done.6 = bf16[2,48,1536]{2,1,0:T(8,128)(2,1)S(1)} collective-permute-done((bf16[2,48,1536]{2,1,0:T(8,128)(2,1)S(1)}, bf16[2,48,1536]{2,1,0:T(8,128)(2,1)S(1)}, u32[]{:S(2)}, u32[]{:S(2)}) %collective-permute-start.6) | collective-permute-done | bytes 294944 | tf_op jit(solution)/shard_map/ppermute | solution.py:271
  42.2 2.6 %collective-permute-done.3 = bf16[2,2,48,1152]{3,2,1,0:T(8,128)(2,1)S(1)} collective-permute-done((bf16[2,2,48,1152]{3,2,1,0:T(8,128)(2,1)S(1)}, bf16[2,2,48,1152]{3,2,1,0:T(8,128)(2,1)S(1)}, u32[]{:S(2)}, u32[]{:S(2)}) %collective-permute-start.3) | collective-permute-done | bytes 442400 | tf_op jit(solution)/shard_map/ppermute | solution.py:271
  48.7 2.8 %maximum_select_fusion.3 = bf16[2,512,768]{2,1,0:T(8,128)(2,1)} fusion(bf16[1,512,768]{2,1,0:T(8,128)(2,1)S(1)} %bitcast.224, bf16[1,512,768]{2,1,0:T(8,128)(2,1)} %bitcast.46, pred[]{:T(512)S(6)} %eq.37), kind=kLoop, calls=%fused_computation.53 | loop fusion | flops 2359296 | bytes 3145729 | tf_op jit(solution)/shard_map/jit(_where)/select_n | solution.py:284
  55.5 2.4 maximum_select_fusion.4
  57.9 2.5 %maximum_select_fusion.5 = bf16[1,2,2,2,48,1536]{5,4,0,1,3,2:T(8,128)(2,1)} fusion(bf16[1,1,2,2,48,1536]{5,4,0,1,3,2:T(8,128)(2,1)S(1)} %copy-done.25, bf16[1,1,2,2,48,1536]{5,4,0,1,3,2:T(8,128)(2,1)} %bitcast.41, pred[]{:T(512)S(6)} %eq.39), kind=kLoop, calls=%fused_computation.60 | loop fusion | flops 1769472 | bytes 2359297 | tf_op jit(solution)/shard_map/jit(_where)/select_n | solution.py:284
  69.9 2.3 copy-done.3
  72.3 11.6 %scan_forward.1 = (f32[1024,768]{1,0:T(8,128)S(1)}, f32[1024,1024]{1,0:T(8,128)S(1)}, bf16[4,128,768]{2,1,0:T(8,128)(2,1)S(1)}) custom-call(f32[1024,1152]{1,0:T(8,128)S(1)} %copy-done.3, f32[1024,128]{1,0:T(8,128)S(1)} %pad.17.col_ref, f32[32,1024]{1,0:T(8,128)S(1)} %copy.166.row_ref, f32[8,1024]{1,0:T(8,128)S(1)} %maximum_maximum_fusion.w_ref, ...), custom_call_target="tpu_custom_call" | custom-call | flops 20000000000 | bytes 13000000 | tf_op jit(solution)/shard_map/scan_forward/pallas_call | solution.py:192
  83.9 2.4 copy.205
  90.7 4.3 %multiply_reduce_fusion.2 = (f32[1024]{0:T(1024)S(1)}, f32[1024]{0:T(1024)S(1)}, f32[1024,768]{1,0:T(8,128)}, f32[1024,768]{1,0:T(8,128)}) fusion(f32[768]{0:T(1024)S(1)} %copy-done.40, f32[1024,768]{1,0:T(8,128)S(1)} %get-tuple-element.24, f32[1024,768]{1,0:T(8,128)S(1)} %fusion.81, bf16[1024,768]{1,0:T(8,128)(2,1)S(1)} %bitcast.238, ...), kind=kOutput, calls=%fused_computation.26 | convolution fusion | flops 1215821824 | bytes 15347712 | tf_op jit(solution)/shard_map/dot_general | solution.py:23
  98.7 2.4 slice.168
  101.2 6.6 %multiply_convert_fusion.1 = (bf16[1024,768]{1,0:T(8,128)(2,1)S(1)}, bf16[1024,768]{1,0:T(8,128)(2,1)}, f32[768]{0:T(1024)S(1)}, bf16[1024,768]{1,0:T(8,128)(2,1)}) fusion(f32[1024,768]{1,0:T(8,128)} %get-tuple-element.131, f32[1024]{0:T(1024)S(1)} %fusion.66, f32[1024,768]{1,0:T(8,128)} %get-tuple-element.171, f32[1024]{0:T(1024)S(1)} %bitcast.250, ...), kind=kLoop, calls=%fused_computation.22 | loop fusion | flops 18087168 | bytes 17315840 | tf_op jit(solution)/shard_map/convert_element_type | solution.py:383
  107.8 27.5 %scan_backward.1 = (bf16[1024,768]{1,0:T(8,128)(2,1)S(1)}, bf16[1024,256]{1,0:T(8,128)(2,1)S(1)}, f32[1024,128]{1,0:T(8,128)S(1)}, f32[16,1024]{1,0:T(8,128)S(1)...) custom-call(f32[1024,1152]{1,0:T(8,128)} %copy-done.2, f32[1024,1024]{1,0:T(8,128)S(1)} %copy-done.5, ...), custom_call_target="tpu_custom_call" | custom-call | flops 40000000000 | bytes 15000000 | tf_op jit(solution)/shard_map/scan_backward/pallas_call | solution.py:229
  140.2 3.5 %fusion.90 = f32[768,768]{0,1:T(8,128)S(1)} fusion(bf16[1024,768]{1,0:T(8,128)(2,1)} %copy-done.13, bf16[1024,768]{1,0:T(8,128)(2,1)} %get-tuple-element.135), kind=kOutput, calls=%fused_computation.193 | convolution fusion | flops 1207959552 | bytes 5505024 | tf_op jit(solution)/shard_map/dot_general | solution.py:23
  145.2 2.5 %pad_maximum_fusion = f32[768,1536]{0,1:T(8,128)} fusion(f32[768,768]{0,1:T(8,128)S(1)} %fusion.91, f32[768,768]{0,1:T(8,128)S(1)} %fusion.90), kind=kLoop, calls=%fused_computation | loop fusion | flops 1179648 | bytes 9437184 | tf_op jit(solution)/shard_map/concatenate | solution.py:392
  147.8 6.4 %copy.183 = f32[768,1536]{1,0:T(8,128)} copy(f32[768,1536]{0,1:T(8,128)} %pad_maximum_fusion) | data formatting | bytes 9437184 | tf_op jit(solution)/shard_map/concatenate | solution.py:392
  157.6 6.5 %fusion.14 = (f32[768]{0:T(1024)S(1)}, f32[1024,768]{1,0:T(8,128)}) fusion(f32[1024]{0:T(1024)S(1)} %bitcast.254, bf16[1,512,768]{2,1,0:T(8,128)(2,1)S(1)} %bitcast.212, bf16[1,512,768]{2,1,0:T(8,128)(2,1)S(1)} %bitcast.205, pred[]{:T(512)S(6)} %eq.37, bf16[768,768]{1,0:T(8,128)(2,1)} %slice.168, bf16[768,1152]{1,0:T(8,128)(2,1)S(1)} %bitcast.234, ...), kind=kOutput, calls=%fused_computation.19 | convolution fusion | flops 3047030016 | bytes 11607041 | tf_op jit(solution)/shard_map/dot_general | solution.py:23
  165.7 2.9 %fusion.29 = bf16[2,2,2,48,1536]{4,3,0,1,2:T(8,128)(2,1)} fusion(f32[2,2,2,2,48,1536]{5,4,3,2,1,0:T(8,128)} %bitcast.206, s32[]{:T(128)S(6)} %select_n.361), kind=kLoop, calls=%fused_computation.58 | loop fusion | bytes 2359300 | tf_op jit(solution)/shard_map/convert_element_type | solution.py:308
  169.3 3.2 %convolution_convert_fusion = bf16[512,768]{1,0:T(8,128)(2,1)} fusion(bf16[768,1536]{1,0:T(8,128)(2,1)} %bitcast.217, bf16[1024,768]{1,0:T(8,128)(2,1)} %get-tuple-element.137, s32[]{:T(128)S(6)} %select_n.359), kind=kOutput, calls=%fused_computation.57 | convolution fusion | flops 604372992 | bytes 2752516 | tf_op jit(solution)/shard_map/dot_general | solution.py:23
  181.0 3.2 %collective-permute-start.18 = (f32[56,128]{1,0:T(8,128)S(1)}, f32[56,128]{1,0:T(8,128)S(1)}, u32[]{:S(2)}, u32[]{:S(2)}) collective-permute-start(f32[56,128]{1,0:T(8,128)S(1)} %add.255), channel_id=1, source_target_pairs={{0,16},{2,18},{4,20},{6,22},{8,24},{10,26},{12,28},{14,30},{16,0},... | collective-permute-start | bytes 86024 | tf_op jit(solution)/shard_map/ppermute | solution.py:271
  184.2 2.4 dynamic-slice_convert_fusion.1
  190.9 2.3 collective-permute-done.11
  193.2 3.1 %fusion.24 = bf16[512,768]{1,0:T(8,128)(2,1)} fusion(bf16[512,768]{1,0:T(8,128)(2,1)S(1)} %copy-done.9, bf16[512,768]{1,0:T(8,128)(2,1)} %collective-permute-done.11, bf16[768,1536]{1,0:T(8,128)(2,1)S(1)} %bitcast.218, bf16[1024,768]{1,0:T(8,128)(2,1)} %get-tuple-element.137, s32[]{:T(128)S(6)} %select_n.358), kind=kOutput, calls=%fused_computation.47 | convolution fusion | flops 605945856 | bytes 4325380 | tf_op jit(solution)/shard_map/dot_general | solution.py:23
  196.3 2.5 %bitcast_add_fusion = f32[2,2,2,48,1536]{4,3,0,1,2:T(8,128)S(1)} fusion(bf16[2,2,2,48,1536]{4,3,0,1,2:T(8,128)(2,1)} %collective-permute-done.19, f32[2,2,2,2,48,1536]{5,4,3,2,1,0:T(8,128)} %bitcast.207, s32[]{:T(128)S(6)} %select_n.360), kind=kLoop, calls=%fused_computation.43 | loop fusion | flops 1179648 | bytes 5898244 | tf_op jit(solution)/shard_map/add | solution.py:309
  200.5 8.8 %collective-permute-done.13 = bf16[512,768]{1,0:T(8,128)(2,1)} collective-permute-done((bf16[512,768]{1,0:T(8,128)(2,1)}, bf16[512,768]{1,0:T(8,128)(2,1)}, u32[]{:S(2)}, u32[]{:S(2)}) %collective-permute-start.13) | collective-permute-done | bytes 786464 | tf_op jit(solution)/shard_map/ppermute | solution.py:271
  210.8 2.8 %fusion.27 = bf16[512,768]{1,0:T(8,128)(2,1)} fusion(bf16[512,768]{1,0:T(8,128)(2,1)S(1)} %copy-done.9, bf16[512,768]{1,0:T(8,128)(2,1)S(1)} %copy-done.24, bf16[512,768]{1,0:T(8,128)(2,1)} %collective-permute-done.13, f32[1024,768]{1,0:T(8,128)S(1)} %copy-done.17, s32[]{:T(128)S(6)} %select_n.358, f32[512]{0:T(512)S(1)} %broadcast_multiply_fusion.2, ...), kind=kLoop, calls=%fused_computation.50 | loop fusion | flops 4325376 | bytes 4727812 | tf_op jit(solution)/shard_map/convert_element_type | solution.py:449
  218.6 7.8 %collective-permute-done.24 = bf16[2,2,48,1152]{3,2,1,0:T(8,128)(2,1)S(1)} collective-permute-done((bf16[2,2,48,1152]{3,2,1,0:T(8,128)(2,1)S(1)}, bf16[2,2,48,1152]{3,2,1,0:T(8,128)(2,1)S(1)}, u32[]{:S(2)}, u32[]{:S(2)}) %collective-permute-start.24) | collective-permute-done | bytes 442400 | tf_op jit(solution)/shard_map/ppermute | solution.py:271
  228.5 4.1 %collective-permute-done.25 = bf16[2,48,1152]{2,1,0:T(8,128)(2,1)S(1)} collective-permute-done((bf16[2,48,1152]{2,1,0:T(8,128)(2,1)S(1)}, bf16[2,48,1152]{2,1,0:T(8,128)(2,1)S(1)}, u32[]{:S(2)}, u32[]{:S(2)}) %collective-permute-start.25) | collective-permute-done | bytes 221216 | tf_op jit(solution)/shard_map/ppermute | solution.py:271
  232.7 3.2 %collective-permute-start.26 = (bf16[48,1152]{1,0:T(8,128)(2,1)S(1)}, bf16[48,1152]{1,0:T(8,128)(2,1)S(1)}, u32[]{:S(2)}, u32[]{:S(2)}) collective-permute-start(bf16[48,1152]{1,0:T(8,128)(2,1)S(1)} %fusion.60), channel_id=1, source_target_pairs={{0,16},{2,18},{4,20},{6,22},{8,24},{10,26},{12,28},{14,30},{16,0},... | collective-permute-start | bytes 331784 | tf_op jit(solution)/shard_map/ppermute | solution.py:271
  236.0 7.7 %collective-permute-done.26 = bf16[48,1152]{1,0:T(8,128)(2,1)S(1)} collective-permute-done((bf16[48,1152]{1,0:T(8,128)(2,1)S(1)}, bf16[48,1152]{1,0:T(8,128)(2,1)S(1)}, u32[]{:S(2)}, u32[]{:S(2)}) %collective-permute-start.26) | collective-permute-done | bytes 110624 | tf_op jit(solution)/shard_map/ppermute | solution.py:271
  (245 shorter events, 79.4 us)
Async XLA Ops:
  0.6 12.4 %copy-start.42 = (f32[12]{0:T(128)S(1)}, f32[12]{0:T(128)}, u32[]{:S(2)}) copy-start(f32[12]{0:T(128)} %param.27) | copy-start | bytes 148
  3.1 10.0 %collective-permute-start.1 = (bf16[48,1152]{1,0:T(8,128)(2,1)S(1)}, bf16[48,1152]{1,0:T(8,128)(2,1)S(1)}, u32[]{:S(2)}, u32[]{:S(2)}) collective-permute-start(bf16[48,1152]{1,0:T(8,128)(2,1)S(1)} %fusion.59), channel_id=1, source_target_pairs={{0,8},{2,10},{4,12},{6,14},{8,0},{10,2},{12,4},{14,6},{16,24},{18,... | collective-permute-start | bytes 331784 | tf_op jit(solution)/shard_map/ppermute | solution.py:271
  6.2 40.8 %collective-permute-start = (bf16[512,768]{1,0:T(8,128)(2,1)}, bf16[512,768]{1,0:T(8,128)(2,1)S(1)}, u32[]{:S(2)}, u32[]{:S(2)}) collective-permute-start(bf16[512,768]{1,0:T(8,128)(2,1)} %param.15), channel_id=1, source_target_pairs={{0,1},{1,0},{2,3},{3,2},{4,5},{5,4},{6,7},{7,6},{8,9},{9,8},{10,11... | collective-permute-start | bytes 2359304 | tf_op jit(solution)/shard_map/ppermute | solution.py:271
  8.6 7.7 %collective-permute-start.5 = (bf16[48,1536]{1,0:T(8,128)(2,1)S(1)}, bf16[48,1536]{1,0:T(8,128)(2,1)S(1)}, u32[]{:S(2)}, u32[]{:S(2)}) collective-permute-start(bf16[48,1536]{1,0:T(8,128)(2,1)S(1)} %get-tuple-element.149), channel_id=1, source_target_pairs={{0,8},{2,10},{4,12},{6,14},{8,0},{10,2},{12,4},{14,6},{16,24},{18,... | collective-permute-start | bytes 442376 | tf_op jit(solution)/shard_map/ppermute | solution.py:271
  9.1 39.1 %collective-permute-start.9 = (bf16[512,768]{1,0:T(8,128)(2,1)}, bf16[512,768]{1,0:T(8,128)(2,1)}, u32[]{:S(2)}, u32[]{:S(2)}) collective-permute-start(bf16[512,768]{1,0:T(8,128)(2,1)} %param.16), channel_id=1, source_target_pairs={{0,1},{1,0},{2,3},{3,2},{4,5},{5,4},{6,7},{7,6},{8,9},{9,8},{10,11... | collective-permute-start | bytes 2359304 | tf_op jit(solution)/shard_map/ppermute | solution.py:271
  13.2 19.6 %collective-permute-start.2 = (bf16[2,48,1152]{2,1,0:T(8,128)(2,1)S(1)}, bf16[2,48,1152]{2,1,0:T(8,128)(2,1)S(1)}, u32[]{:S(2)}, u32[]{:S(2)}) collective-permute-start(bf16[2,48,1152]{2,1,0:T(8,128)(2,1)S(1)} %maximum_select_fusion.14), channel_id=1, source_target_pairs={{0,16},{2,18},{4,20},{6,22},{8,24},{10,26},{12,28},{14,30},{16,0},... | collective-permute-start | bytes 663560 | tf_op jit(solution)/shard_map/ppermute | solution.py:271
  16.4 21.6 %collective-permute-start.6 = (bf16[2,48,1536]{2,1,0:T(8,128)(2,1)S(1)}, bf16[2,48,1536]{2,1,0:T(8,128)(2,1)S(1)}, u32[]{:S(2)}, u32[]{:S(2)}) collective-permute-start(bf16[2,48,1536]{2,1,0:T(8,128)(2,1)S(1)} %maximum_select_fusion.12), channel_id=1, source_target_pairs={{0,16},{2,18},{4,20},{6,22},{8,24},{10,26},{12,28},{14,30},{16,0},... | collective-permute-start | bytes 884744 | tf_op jit(solution)/shard_map/ppermute | solution.py:271
  32.9 11.9 %collective-permute-start.3 = (bf16[2,2,48,1152]{3,2,1,0:T(8,128)(2,1)S(1)}, bf16[2,2,48,1152]{3,2,1,0:T(8,128)(2,1)S(1)}, u32[]{:S(2)}, u32[]{:S(2)}) collective-permute-start(bf16[2,2,48,1152]{3,2,1,0:T(8,128)(2,1)S(1)} %maximum_select_fusion.10), channel_id=1, source_target_pairs={{0,4},{2,6},{4,0},{6,2},{8,12},{10,14},{12,8},{14,10},{16,20},{18,... | collective-permute-start | bytes 1327112 | tf_op jit(solution)/shard_map/ppermute | solution.py:271
  38.8 16.6 %collective-permute-start.7 = (bf16[2,2,48,1536]{3,2,1,0:T(8,128)(2,1)}, bf16[2,2,48,1536]{3,2,1,0:T(8,128)(2,1)}, u32[]{:S(2)}, u32[]{:S(2)}) collective-permute-start(bf16[2,2,48,1536]{3,2,1,0:T(8,128)(2,1)} %maximum_select_fusion.8), channel_id=1, source_target_pairs={{0,4},{2,6},{4,0},{6,2},{8,12},{10,14},{12,8},{14,10},{16,20},{18,... | collective-permute-start | bytes 1769480 | tf_op jit(solution)/shard_map/ppermute | solution.py:271
  45.9 14.6 %collective-permute-start.4 = (bf16[2,2,2,48,1152]{4,3,2,1,0:T(8,128)(2,1)}, bf16[2,2,2,48,1152]{4,3,2,1,0:T(8,128)(2,1)}, u32[]{:S(2)}, u32[]{:S(2)}) collective-permute-start(bf16[2,2,2,48,1152]{4,3,2,1,0:T(8,128)(2,1)} %maximum_select_fusion.6), channel_id=1, source_target_pairs={{0,2},{2,0},{4,6},{6,4},{8,10},{10,8},{12,14},{14,12},{16,18},{18,... | collective-permute-start | bytes 2654216 | tf_op jit(solution)/shard_map/ppermute | solution.py:271
  57.9 26.0 %collective-permute-start.8 = (bf16[2,2,2,48,1536]{4,3,2,1,0:T(8,128)(2,1)}, bf16[2,2,2,48,1536]{4,3,2,1,0:T(8,128)(2,1)}, u32[]{:S(2)}, u32[]{:S(2)}) collective-permute-start(bf16[2,2,2,48,1536]{4,3,2,1,0:T(8,128)(2,1)} %maximum_select_fusion.4), channel_id=1, source_target_pairs={{0,2},{2,0},{4,6},{6,4},{8,10},{10,8},{12,14},{14,12},{16,18},{18,... | collective-permute-start | bytes 3538952 | tf_op jit(solution)/shard_map/ppermute | solution.py:271
  72.2 11.6 %copy-start = (f32[1024,128]{1,0:T(8,128)}, f32[1024,128]{1,0:T(8,128)S(1)}, u32[]{:S(2)}) copy-start(f32[1024,128]{1,0:T(8,128)S(1)} %pad.17.col_ref) | copy-start | bytes 1572868
  95.1 6.0 %collective-permute-start.10 = (f32[2,1024]{1,0:T(2,128)S(1)}, f32[2,1024]{1,0:T(2,128)S(1)}, u32[]{:S(2)}, u32[]{:S(2)}) collective-permute-start(f32[2,1024]{1,0:T(2,128)S(1)} %pad_maximum_fusion.5), channel_id=1, source_target_pairs={{0,1},{1,0},{2,3},{3,2},{4,5},{5,4},{6,7},{7,6},{8,9},{9,8},{10,11... | collective-permute-start | bytes 24584 | tf_op jit(solution)/shard_map/ppermute | solution.py:271
  135.3 20.7 %collective-permute-start.12 = (bf16[1024,256]{1,0:T(8,128)(2,1)S(1)}, bf16[1024,256]{1,0:T(8,128)(2,1)}, u32[]{:S(2)}, u32[]{:S(2)}) collective-permute-start(bf16[1024,256]{1,0:T(8,128)(2,1)S(1)} %get-tuple-element.28), channel_id=1, source_target_pairs={{0,1},{1,0},{2,3},{3,2},{4,5},{5,4},{6,7},{7,6},{8,9},{9,8},{10,11... | collective-permute-start | bytes 1572872 | tf_op jit(solution)/shard_map/ppermute | solution.py:271
  164.1 4.5 %collective-permute-start.14 = (f32[2048]{0:T(1024)S(1)}, f32[2048]{0:T(1024)S(1)}, u32[]{:S(2)}, u32[]{:S(2)}) collective-permute-start(f32[2048]{0:T(1024)S(1)} %pad_maximum_fusion.6), channel_id=1, source_target_pairs={{0,1},{1,0},{2,3},{3,2},{4,5},{5,4},{6,7},{7,6},{8,9},{9,8},{10,11... | collective-permute-start | bytes 24584 | tf_op jit(solution)/shard_map/ppermute | solution.py:271
  168.6 27.7 %collective-permute-start.19 = (bf16[2,2,2,48,1536]{4,3,0,1,2:T(8,128)(2,1)}, bf16[2,2,2,48,1536]{4,3,0,1,2:T(8,128)(2,1)}, u32[]{:S(2)}, u32[]{:S(2)}) collective-permute-start(bf16[2,2,2,48,1536]{4,3,0,1,2:T(8,128)(2,1)} %fusion.29), channel_id=1, source_target_pairs={{0,2},{2,0},{4,6},{6,4},{8,10},{10,8},{12,14},{14,12},{16,18},{18,... | collective-permute-start | bytes 3538952 | tf_op jit(solution)/shard_map/ppermute | solution.py:271
  168.7 4.3 %collective-permute-start.15 = (f32[56,128]{1,0:T(8,128)S(1)}, f32[56,128]{1,0:T(8,128)S(1)}, u32[]{:S(2)}, u32[]{:S(2)}) collective-permute-start(f32[56,128]{1,0:T(8,128)S(1)} %pad_bitcast_fusion), channel_id=1, source_target_pairs={{0,2},{2,0},{4,6},{6,4},{8,10},{10,8},{12,14},{14,12},{16,18},{18,... | collective-permute-start | bytes 86024 | tf_op jit(solution)/shard_map/ppermute | solution.py:271
  172.5 20.7 %collective-permute-start.11 = (bf16[512,768]{1,0:T(8,128)(2,1)}, bf16[512,768]{1,0:T(8,128)(2,1)}, u32[]{:S(2)}, u32[]{:S(2)}) collective-permute-start(bf16[512,768]{1,0:T(8,128)(2,1)} %convolution_convert_fusion), channel_id=1, source_target_pairs={{0,1},{1,0},{2,3},{3,2},{4,5},{5,4},{6,7},{7,6},{8,9},{9,8},{10,11... | collective-permute-start | bytes 2359304 | tf_op jit(solution)/shard_map/ppermute | solution.py:271
  173.1 4.0 %collective-permute-start.16 = (f32[56,128]{1,0:T(8,128)S(1)}, f32[56,128]{1,0:T(8,128)S(1)}, u32[]{:S(2)}, u32[]{:S(2)}) collective-permute-start(f32[56,128]{1,0:T(8,128)S(1)} %fusion.75), channel_id=1, source_target_pairs={{0,4},{2,6},{4,0},{6,2},{8,12},{10,14},{12,8},{14,10},{16,20},{18,... | collective-permute-start | bytes 86024 | tf_op jit(solution)/shard_map/ppermute | solution.py:271
  177.1 16.2 %copy-start.16 = (bf16[2,2,2,2,48,1536]{5,4,0,1,3,2:T(8,128)(2,1)S(1)}, bf16[2,2,2,2,48,1536]{5,4,0,1,3,2:T(8,128)(2,1)}, u32[]{:S(2)}) copy-start(bf16[2,2,2,2,48,1536]{5,4,0,1,3,2:T(8,128)(2,1)} %copy-done.15) | copy-start | bytes 7077892
  177.1 3.9 %collective-permute-start.17 = (f32[56,128]{1,0:T(8,128)S(1)}, f32[56,128]{1,0:T(8,128)S(1)}, u32[]{:S(2)}, u32[]{:S(2)}) collective-permute-start(f32[56,128]{1,0:T(8,128)S(1)} %fusion.102), channel_id=1, source_target_pairs={{0,8},{2,10},{4,12},{6,14},{8,0},{10,2},{12,4},{14,6},{16,24},{18,... | collective-permute-start | bytes 86024 | tf_op jit(solution)/shard_map/ppermute | solution.py:271
  180.0 33.6 %collective-permute-start.23 = (bf16[2,2,2,48,1152]{4,3,2,1,0:T(8,128)(2,1)}, bf16[2,2,2,48,1152]{4,3,2,1,0:T(8,128)(2,1)}, u32[]{:S(2)}, u32[]{:S(2)}) collective-permute-start(bf16[2,2,2,48,1152]{4,3,2,1,0:T(8,128)(2,1)} %fusion.38), channel_id=1, source_target_pairs={{0,2},{2,0},{4,6},{6,4},{8,10},{10,8},{12,14},{14,12},{16,18},{18,... | collective-permute-start | bytes 2654216 | tf_op jit(solution)/shard_map/ppermute | solution.py:271
  181.0 6.9 %collective-permute-start.18 = (f32[56,128]{1,0:T(8,128)S(1)}, f32[56,128]{1,0:T(8,128)S(1)}, u32[]{:S(2)}, u32[]{:S(2)}) collective-permute-start(f32[56,128]{1,0:T(8,128)S(1)} %add.255), channel_id=1, source_target_pairs={{0,16},{2,18},{4,20},{6,22},{8,24},{10,26},{12,28},{14,30},{16,0},... | collective-permute-start | bytes 86024 | tf_op jit(solution)/shard_map/ppermute | solution.py:271
  186.6 22.7 %collective-permute-start.13 = (bf16[512,768]{1,0:T(8,128)(2,1)}, bf16[512,768]{1,0:T(8,128)(2,1)}, u32[]{:S(2)}, u32[]{:S(2)}) collective-permute-start(bf16[512,768]{1,0:T(8,128)(2,1)} %dynamic-slice_convert_fusion.1), channel_id=1, source_target_pairs={{0,1},{1,0},{2,3},{3,2},{4,5},{5,4},{6,7},{7,6},{8,9},{9,8},{10,11... | collective-permute-start | bytes 2359304 | tf_op jit(solution)/shard_map/ppermute | solution.py:271
  196.3 13.0 %copy-start.17 = (f32[1024,768]{1,0:T(8,128)S(1)}, f32[1024,768]{1,0:T(8,128)}, u32[]{:S(2)}) copy-start(f32[1024,768]{1,0:T(8,128)} %get-tuple-element.173) | copy-start | bytes 9437188
  198.9 11.9 %copy-start.24 = (bf16[512,768]{1,0:T(8,128)(2,1)S(1)}, bf16[512,768]{1,0:T(8,128)(2,1)}, u32[]{:S(2)}) copy-start(bf16[512,768]{1,0:T(8,128)(2,1)} %param.16) | copy-start | bytes 2359300
  198.9 17.7 %collective-permute-start.20 = (bf16[2,2,48,1536]{3,2,0,1:T(8,128)(2,1)S(1)}, bf16[2,2,48,1536]{3,2,0,1:T(8,128)(2,1)S(1)}, u32[]{:S(2)}, u32[]{:S(2)}) collective-permute-start(bf16[2,2,48,1536]{3,2,0,1:T(8,128)(2,1)S(1)} %fusion.41), channel_id=1, source_target_pairs={{0,4},{2,6},{4,0},{6,2},{8,12},{10,14},{12,8},{14,10},{16,20},{18,... | collective-permute-start | bytes 1769480 | tf_op jit(solution)/shard_map/ppermute | solution.py:271
  215.0 11.4 %collective-permute-start.24 = (bf16[2,2,48,1152]{3,2,1,0:T(8,128)(2,1)S(1)}, bf16[2,2,48,1152]{3,2,1,0:T(8,128)(2,1)S(1)}, u32[]{:S(2)}, u32[]{:S(2)}) collective-permute-start(bf16[2,2,48,1152]{3,2,1,0:T(8,128)(2,1)S(1)} %fusion.46), channel_id=1, source_target_pairs={{0,4},{2,6},{4,0},{6,2},{8,12},{10,14},{12,8},{14,10},{16,20},{18,... | collective-permute-start | bytes 1327112 | tf_op jit(solution)/shard_map/ppermute | solution.py:271
  216.8 11.6 %collective-permute-start.21 = (bf16[2,48,1536]{2,1,0:T(8,128)(2,1)S(1)}, bf16[2,48,1536]{2,1,0:T(8,128)(2,1)S(1)}, u32[]{:S(2)}, u32[]{:S(2)}) collective-permute-start(bf16[2,48,1536]{2,1,0:T(8,128)(2,1)S(1)} %fusion.47), channel_id=1, source_target_pairs={{0,8},{2,10},{4,12},{6,14},{8,0},{10,2},{12,4},{14,6},{16,24},{18,... | collective-permute-start | bytes 884744 | tf_op jit(solution)/shard_map/ppermute | solution.py:271
  226.6 6.0 %collective-permute-start.25 = (bf16[2,48,1152]{2,1,0:T(8,128)(2,1)S(1)}, bf16[2,48,1152]{2,1,0:T(8,128)(2,1)S(1)}, u32[]{:S(2)}, u32[]{:S(2)}) collective-permute-start(bf16[2,48,1152]{2,1,0:T(8,128)(2,1)S(1)} %fusion.52), channel_id=1, source_target_pairs={{0,8},{2,10},{4,12},{6,14},{8,0},{10,2},{12,4},{14,6},{16,24},{18,... | collective-permute-start | bytes 663560 | tf_op jit(solution)/shard_map/ppermute | solution.py:271
  232.7 11.1 %collective-permute-start.26 = (bf16[48,1152]{1,0:T(8,128)(2,1)S(1)}, bf16[48,1152]{1,0:T(8,128)(2,1)S(1)}, u32[]{:S(2)}, u32[]{:S(2)}) collective-permute-start(bf16[48,1152]{1,0:T(8,128)(2,1)S(1)} %fusion.60), channel_id=1, source_target_pairs={{0,16},{2,18},{4,20},{6,22},{8,24},{10,26},{12,28},{14,30},{16,0},... | collective-permute-start | bytes 331784 | tf_op jit(solution)/shard_map/ppermute | solution.py:271
  235.9 9.4 %collective-permute-start.22 = (bf16[48,1536]{1,0:T(8,128)(2,1)S(1)}, bf16[48,1536]{1,0:T(8,128)(2,1)S(1)}, u32[]{:S(2)}, u32[]{:S(2)}) collective-permute-start(bf16[48,1536]{1,0:T(8,128)(2,1)S(1)} %fusion.54), channel_id=1, source_target_pairs={{0,16},{2,18},{4,20},{6,22},{8,24},{10,26},{12,28},{14,30},{16,0},... | collective-permute-start | bytes 442376 | tf_op jit(solution)/shard_map/ppermute | solution.py:271
  (38 other events, 139.9 us)

commit v2 on v1

--- a/solution.py
+++ b/solution.py
@@ -27,7 +27,7 @@
     return ref[pl.ds(first, count), columns]
 
 
-def scan_forward(heads, taps, xp_ref, col_ref, row_ref, w_ref, skip_ref, mixed_ref, pre_ref, states_ref, buf, act, st):
+def scan_forward(heads, taps, xp_ref, col_ref, row_ref, w_ref, skip_ref, _, mixed_ref, pre_ref, states_ref, buf, act, st):
     channels = skip_ref.shape[1]
     wide = xp_ref.shape[1]
     state_size = (wide - channels) // 2
@@ -80,18 +80,19 @@
 
 
 def scan_backward(
-    heads, taps, xp_ref, pre_ref, col_ref, row_ref, w_ref, skip_ref, states_ref, dy_ref,
-    dx_ref, dbc_ref, colout_ref, rowout_ref, sums_ref, gw_ref, buf, dst, dgs,
+    heads, taps, passed, xp_ref, pre_ref, col_ref, row_ref, w_ref, skip_ref, states_ref, dy_ref,
+    gw_in, dst_in, carry_in, *refs,
 ):
+    dx_ref, dbc_ref, colout_ref, rowout_ref, sums_ref, gw_ref, dst_out, carry_out, buf, dst, dgs = refs[passed:]
     channels = skip_ref.shape[1]
     wide = xp_ref.shape[1]
     state_size = (wide - channels) // 2
 
     @pl.when(pl.program_id(0) == 0)
     def _():
-        dst[...] = jnp.zeros_like(dst)
-        buf[Q : Q + 8, :] = jnp.zeros((8, wide), F32)
-        gw_ref[...] = jnp.zeros_like(gw_ref)
+        dst[...] = dst_in[...]
+        buf[Q : Q + 8, :] = carry_in[...]
+        gw_ref[...] = gw_in[...]
 
     def act_of(start):
         pre = pre_ref[:, pl.ds(start, LANES)]
@@ -179,12 +180,17 @@
     dbc_ref[:, :state_size] = conv_back(channels, d_inject)
     dbc_ref[:, state_size:] = conv_back(channels + state_size, d_readout)
 
+    @pl.when(pl.program_id(0) == pl.num_programs(0) - 1)
+    def _():
+        dst_out[...] = dst[...]
+        carry_out[...] = buf[Q : Q + 8, :]
+
 
 def whole_block(shape):
     return pl.BlockSpec(shape, lambda i: (0,) * len(shape))
 
 
-def run_forward(xp, col, row, w, skip, heads, taps):
+def run_forward(xp, col, row, w, skip, heads, taps, after):
     length, wide = xp.shape[0], w.shape[1]
     channels = skip.shape[1]
     chunks = length // Q
@@ -198,6 +204,7 @@
             pl.BlockSpec((2 * DT_AT, Q), lambda i: (0, i)),
             whole_block(w.shape),
             whole_block(skip.shape),
+            pl.BlockSpec(memory_space=pl.ANY),
         ],
         out_specs=[
             pl.BlockSpec((Q, channels), lambda i: (i, 0)),
@@ -217,35 +224,50 @@
         compiler_params=pltpu.CompilerParams(vmem_limit_bytes=40 * 2**20),
         cost_estimate=pl.CostEstimate(flops=20 * 10**9, bytes_accessed=13 * 10**6, transcendentals=5 * 10**6),
         name="scan_forward",
-    )(xp, col, row, w, skip)
-
-
-def run_backward(xp, pre, col, row, w, skip, states, dy, heads, taps):
+    )(xp, col, row, w, skip, after)
+
+
+def run_backward(low, high, kept, after, xp, pre, col, row, w, skip, states, dy, heads, taps):
     length, wide = pre.shape
     channels = skip.shape[1]
     chunks = length // Q
     state_size = (wide - channels) // 2
-    back = lambda i: (chunks - 1 - i, 0)
+    back = lambda i: (high - 1 - i, 0)
+    across = lambda i: (0, high - 1 - i)
+    first = lambda i: (high - 1 - i, 0, 0)
+    if kept is None:
+        buffers = []
+        carries = [jnp.zeros(w.shape, F32), jnp.zeros((state_size, channels), F32), jnp.zeros((8, wide), F32)]
+    else:
+        buffers, carries = list(kept[:5]), list(kept[5:])
+    anywhere = pl.BlockSpec(memory_space=pl.ANY)
+    passed = len(buffers) + len(after)
     return pl.pallas_call(
-        functools.partial(scan_backward, heads, taps),
-        grid=(chunks,),
+        functools.partial(scan_backward, heads, taps, passed),
+        grid=(high - low,),
         in_specs=[
             pl.BlockSpec((Q, wide), back),
             pl.BlockSpec((Q, wide), back),
             pl.BlockSpec((Q, LANES), back),
-            pl.BlockSpec((2 * DT_AT, Q), lambda i: (0, chunks - 1 - i)),
+            pl.BlockSpec((2 * DT_AT, Q), across),
             whole_block(w.shape),
             whole_block(skip.shape),
-            pl.BlockSpec((1, state_size, channels), lambda i: (chunks - 1 - i, 0, 0)),
+            pl.BlockSpec((1, state_size, channels), first),
             pl.BlockSpec((Q, channels), back),
-        ],
+            whole_block(w.shape),
+            whole_block((state_size, channels)),
+            whole_block((8, wide)),
+        ]
+        + [anywhere] * passed,
         out_specs=[
             pl.BlockSpec((Q, channels), back),
             pl.BlockSpec((Q, 2 * state_size), back),
             pl.BlockSpec((Q, LANES), back),
-            pl.BlockSpec((DT_AT, Q), lambda i: (0, chunks - 1 - i)),
-            pl.BlockSpec((1, 2, channels), lambda i: (chunks - 1 - i, 0, 0)),
+            pl.BlockSpec((DT_AT, Q), across),
+            pl.BlockSpec((1, 2, channels), first),
             whole_block(w.shape),
+            whole_block((state_size, channels)),
+            whole_block((8, wide)),
         ],
         out_shape=[
             jax.ShapeDtypeStruct((length, channels), BF16),
@@ -254,16 +276,21 @@
             jax.ShapeDtypeStruct((DT_AT, length), F32),
             jax.ShapeDtypeStruct((chunks, 2, channels), F32),
             jax.ShapeDtypeStruct(w.shape, F32),
+            jax.ShapeDtypeStruct((state_size, channels), F32),
+            jax.ShapeDtypeStruct((8, wide), F32),
         ],
         scratch_shapes=[
             pltpu.VMEM((Q + 8, wide), F32),
             pltpu.VMEM((state_size, channels), F32),
             pltpu.VMEM((Q, Q), F32),
         ],
+        input_output_aliases={11 + k: k for k in range(len(buffers))},
         compiler_params=pltpu.CompilerParams(vmem_limit_bytes=40 * 2**20),
-        cost_estimate=pl.CostEstimate(flops=40 * 10**9, bytes_accessed=15 * 10**6, transcendentals=5 * 10**6),
+        cost_estimate=pl.CostEstimate(
+            flops=(high - low) * 8 * 10**9, bytes_accessed=(high - low) * 4 * 10**6, transcendentals=10**6
+        ),
         name="scan_backward",
-    )(xp, pre, col, row, w, skip, states, dy)
+    )(xp, pre, col, row, w, skip, states, dy, *carries, *buffers, *after)
 
 
 def swap(x, axis, bit):
@@ -284,31 +311,33 @@
     return jnp.where(second == 1, jnp.stack([other, own]), jnp.stack([own, other]))
 
 
-def gather_rows(block):
+def gather_rows(block, order):
     bits = bits_of("dp")
-    order = [b for b in bits if b > 2] + [b for b in bits if b == 2] + [b for b in bits if b == 1]
     x = block
     for bit in order:
+        last = x
         x = both(x, swap(x, "dp", bit), my_bit("dp", bit))
     done = order[::-1]
     axes = [done.index(b) for b in bits[::-1]]
     count = len(bits)
     x = jnp.transpose(x, axes + list(range(count, count + block.ndim)))
-    return x.reshape((-1,) + block.shape[1:])
-
-
-def scatter_rows(x):
+    return x.reshape((-1,) + block.shape[1:]), last
+
+
+def scatter_rows(parts):
     bits = bits_of("dp")
     left = bits[::-1]
-    x = x.reshape((2,) * len(bits) + (x.shape[0] >> len(bits), x.shape[1]))
+    parts = [x.reshape((2,) * len(bits) + (x.shape[0] >> len(bits), x.shape[1])) for x in parts]
     for bit in bits:
         axis = left.index(bit)
         mine = my_bit("dp", bit)
-        keep = lax.dynamic_index_in_dim(x, mine, axis, keepdims=False)
-        send = lax.dynamic_index_in_dim(x, 1 - mine, axis, keepdims=False).astype(BF16)
-        x = keep.astype(F32) + swap(send, "dp", bit).astype(F32)
+        keep = [lax.dynamic_index_in_dim(x, mine, axis, keepdims=False) for x in parts]
+        send = [lax.dynamic_index_in_dim(x, 1 - mine, axis, keepdims=False).astype(BF16) for x in parts]
+        keep, send = (jnp.concatenate(x, axis=-1) if len(x) > 1 else x[0] for x in (keep, send))
+        yield send
+        parts = [keep + swap(send, "dp", bit).astype(F32)]
         left.remove(bit)
-    return x
+    yield parts[0]
 
 
 def sum_dp(x):
@@ -338,10 +367,15 @@
         return lax.dynamic_slice_in_dim(x, (1 - side) * own_rows, own_rows, 0)
 
     pad_dt = LANES - heads
-    weights_in = gather_rows(
-        jnp.concatenate([w_zx[1], w_bc[0], w_bc[1], jnp.pad(w_dt, ((0, 0), (0, pad_dt)))], axis=1)
-    )
-    weights_side = gather_rows(jnp.concatenate([w_zx[0], w_out.T], axis=1))
+    bits = bits_of("dp")
+    far = bits[:1:-1]
+    weights_in, _ = gather_rows(
+        jnp.concatenate([w_zx[1], w_bc[0], w_bc[1], jnp.pad(w_dt, ((0, 0), (0, pad_dt)))], axis=1),
+        far + bits[1:2] + bits[:1],
+    )
+    weights_side, side_last = gather_rows(
+        jnp.concatenate([w_zx[0], w_out.T], axis=1), bits[1:2] + far + bits[:1]
+    )
     weight_gate, weight_out_t = weights_side[:, :channels], weights_side[:, channels:]
 
     rows = both(residual, swap(residual, "tensor", 1), side).reshape(2 * own_rows, width).astype(F32)
@@ -367,7 +401,7 @@
     bias_all = jnp.concatenate([conv_x_bias, conv_bc_bias[0], conv_bc_bias[1]])
     w = jnp.concatenate([taps_all, bias_all[None], jnp.zeros((8 - taps - 1, wide), F32)], axis=0)
     skip = jnp.repeat(d_skip, head_size)[None]
-    mixed, pre, states = run_forward(projected, col, row, w, skip, heads, taps)
+    mixed, pre, states = run_forward(projected, col, row, w, skip, heads, taps, side_last)
 
     gate_pre = dot(normed, weight_gate)
     d_gated = dot(cotangent, weight_out_t)
@@ -388,12 +422,16 @@
     branch = dot(own_half(gated), weight_out_t, NT) + sent.astype(F32)
     layer_out = (residual.astype(F32) + branch).astype(BF16)
 
-    grad_side = scatter_rows(
-        jnp.concatenate([dot(normed, d_gate, TN), dot(cotangent, gated, TN)], axis=1)
-    )
-    d_x, d_bc, colout, rowout, chunk_sums, grad_w = run_backward(
-        projected, pre, col, row, w, skip, states, d_mixed, heads, taps
-    )
+    steps_side = scatter_rows([dot(normed, d_gate, TN), dot(cotangent, gated, TN)])
+    ends = [0] + [chunks * k // 4 for k in range(1, 5)]
+    kept = None
+    for low, high in ((ends[3], ends[4]), (ends[1], ends[3]), (ends[0], ends[1])):
+        if high > low:
+            kept = run_backward(
+                low, high, kept, [next(steps_side)], projected, pre, col, row, w, skip, states, d_mixed, heads, taps
+            )
+    d_x, d_bc, colout, rowout, chunk_sums, grad_w = kept[:6]
+    *_, grad_side = steps_side
 
     along = colout[:, :heads].reshape(chunks, Q, heads)
     ended = colout[:, DT_AT : DT_AT + heads].reshape(chunks, Q, heads)
@@ -414,10 +452,14 @@
     d_shared = d_bc.astype(F32) + swap(d_bc, "tensor", 1).astype(F32)
     d_shared = d_shared.astype(BF16)
     d_dt_low = jnp.pad(d_dt.astype(BF16), ((0, 0), (0, pad_dt)))
-    grad_in = scatter_rows(dot(normed, jnp.concatenate([d_x, d_shared, d_dt_low], axis=1), TN))
-    d_all = jnp.concatenate([d_x, d_shared * 0.5, d_dt_low, d_gate], axis=1)
-    weights_all = jnp.concatenate([weights_in, weight_gate], axis=1)
-    partial = dot(d_all, weights_all, NT)
+    d_rest = jnp.concatenate([d_shared, d_dt_low], axis=1)
+    d_rest_half = jnp.concatenate([d_shared * 0.5, d_dt_low], axis=1)
+    *_, grad_in = scatter_rows([dot(normed, d_x, TN), dot(normed, d_rest, TN)])
+    partial = (
+        dot(d_gate, weight_gate, NT)
+        + dot(d_x, weights_in[:, :channels], NT)
+        + dot(d_rest_half, weights_in[:, channels:], NT)
+    )
     received = swap(other_half(partial).astype(BF16), "tensor", 1)
     grad_norm_gain = jnp.sum(partial * rows * in_scale, axis=0)
 

time: 251 us -> 240 us (0.956)
  local copies, waits for them, and re-layouts: 44.5 us -> 33.6 us
  starting transfers between devices: 34.8 us -> 28.9 us
  Pallas kernels: 39.1 us -> 44.1 us
  other arithmetic: 41.9 us -> 38.4 us
    concatenate x1, local copies, waits for them, and re-layouts: 6.37 us -> 0.09 us  [scatter_rows(): jnp.concatenate(x, axis=-1)]
    ppermute x27, starting transfers between devices: 34.8 us -> 28.9 us  [swap(): return lax.ppermute(x, axis, [(i, i ^ bit) for i in range(size)])]
    pallas_call x1 -> x3, Pallas kernels: 27.5 us -> 31.3 us  [run_backward(): pl.pallas_call(functools.partial(scan_backward, heads, taps, passed), gri...]
    transpose x0 -> x1, other arithmetic: none -> 3.5 us  [gather_rows(): x = jnp.transpose(x, axes + list(range(count, count + block.ndim)))]
    slice x2, local copies, waits for them, and re-layouts: 3.35 us -> 0.23 us  [the longest x1 0.2 us: body(): along = colout[:, :heads].reshape(chunks, Q, heads)]
    dot_general x1 -> x2, local copies, waits for them, and re-layouts: 1.78 us -> 4.47 us  [dot(): return lax.dot_general(a, b, dims, preferred_element_type=F32)]
    squeeze x0 -> x3, local copies, waits for them, and re-layouts: none -> 2.56 us  [scatter_rows(): lax.dynamic_index_in_dim(x, mine, axis, keepdims=False)]
    dot_general x9 -> x12, matrix products: 27.9 us -> 30.2 us  [dot(): return lax.dot_general(a, b, dims, preferred_element_type=F32)]
  transfers between devices with their start and end apart: 27 -> 27, of which waited for: 11 -> 16; matrix products, arithmetic and copies ran while one was open for 32% -> 25% of each run, Pallas kernels for 5% -> 19%
where the time goes in v2:
time: 240 us; the launch traced here: 235 us
  waiting for transfers between devices  56.7 us (24%)
  Pallas kernels  44.1 us (18%)
  other arithmetic  38.4 us (16%)
  local copies, waits for them, and re-layouts  33.6 us (14%)
  matrix products  31.6 us (13%)
  starting transfers between devices  28.9 us (12%)
    ppermute x27, waiting for transfers between devices, swap(): return lax.ppermute(x, axis, [(i, i ^ bit) for i in range(size)])  56.7 us
    pallas_call x3, Pallas kernels, run_backward(): pl.pallas_call(functools.partial(scan_backward, heads, taps, passed), gri...  31.3 us
    dot_general x12, matrix products, dot(): return lax.dot_general(a, b, dims, preferred_element_type=F32)  30.2 us
    ppermute x27, starting transfers between devices, swap(): return lax.ppermute(x, axis, [(i, i ^ bit) for i in range(size)])  28.9 us
    unnamed x118, local copies, waits for them, and re-layouts  12.9 us
    pallas_call x1, Pallas kernels, run_forward(): pl.pallas_call(functools.partial(scan_forward, heads, taps), grid=(chunks...  12.8 us
    select_n x14, other arithmetic, both(): jnp.where(second == 1, jnp.stack([other, own]), jnp.stack([own, other]))  12.2 us
    convert_element_type x1, other arithmetic, body(): d_mixed = (d_inner * gate_act).astype(BF16)  6.18 us
  transfers between devices with their start and end apart: 27, of which 16 were waited for; matrix products, arithmetic and copies ran while one was open for 25% of the time, Pallas kernels for 19%

profile of v2, /device:TPU:0, one launch (start us, length us, event | category | flops | bytes accessed | tf_op | source)
XLA Modules:
  0.0 235.4 jit_solution(1190428626660418213)
XLA Ops:
  3.2 4.1 %collective-permute-start.1 = (bf16[48,1152]{1,0:T(8,128)(2,1)S(1)}, bf16[48,1152]{1,0:T(8,128)(2,1)S(1)}, u32[]{:S(2)}, u32[]{:S(2)}) collective-permute-start(bf16[48,1152]{1,0:T(8,128)(2,1)S(1)} %fusion.66), channel_id=1, source_target_pairs={{0,16},{2,18},{4,20},{6,22},{8,24},{10,26},{12,28},{14,30},{16,0},... | collective-permute-start | bytes 331784 | tf_op jit(solution)/shard_map/ppermute | solution.py:298
  15.0 2.2 collective-permute-start.6
  17.2 6.6 %collective-permute-done.2 = bf16[2,48,1152]{2,1,0:T(8,128)(2,1)S(1)} collective-permute-done((bf16[2,48,1152]{2,1,0:T(8,128)(2,1)S(1)}, bf16[2,48,1152]{2,1,0:T(8,128)(2,1)S(1)}, u32[]{:S(2)}, u32[]{:S(2)}) %collective-permute-start.2) | collective-permute-done | bytes 221216 | tf_op jit(solution)/shard_map/ppermute | solution.py:298
  25.3 5.1 %collective-permute-done.6 = bf16[2,48,1536]{2,1,0:T(8,128)(2,1)S(1)} collective-permute-done((bf16[2,48,1536]{2,1,0:T(8,128)(2,1)S(1)}, bf16[2,48,1536]{2,1,0:T(8,128)(2,1)S(1)}, u32[]{:S(2)}, u32[]{:S(2)}) %collective-permute-start.6) | collective-permute-done | bytes 294944 | tf_op jit(solution)/shard_map/ppermute | solution.py:298
  36.6 6.9 %collective-permute-done.9 = bf16[512,768]{1,0:T(8,128)(2,1)} collective-permute-done((bf16[512,768]{1,0:T(8,128)(2,1)}, bf16[512,768]{1,0:T(8,128)(2,1)}, u32[]{:S(2)}, u32[]{:S(2)}) %collective-permute-start.9) | collective-permute-done | bytes 786464 | tf_op jit(solution)/shard_map/ppermute | solution.py:298
  43.5 2.8 %maximum_select_fusion.3 = bf16[2,512,768]{2,1,0:T(8,128)(2,1)} fusion(bf16[1,512,768]{2,1,0:T(8,128)(2,1)S(1)} %bitcast.258, bf16[1,512,768]{2,1,0:T(8,128)(2,1)} %bitcast.46, pred[]{:T(512)S(6)} %eq.37), kind=kLoop, calls=%fused_computation.36 | loop fusion | flops 2359296 | bytes 3145729 | tf_op jit(solution)/shard_map/jit(_where)/select_n | solution.py:311
  48.1 2.6 %copy.134 = bf16[768,1024]{1,0:T(8,128)(2,1)} copy(bf16[768,1024]{0,1:T(8,128)(2,1)} %bitcast.254) | data formatting | bytes 3145728 | tf_op jit(solution)/shard_map/dot_general | solution.py:23
  51.8 2.5 %maximum_select_fusion.4._ = bf16[2,2,2,48,1536]{4,3,2,1,0:T(8,128)(2,1)} fusion(bf16[1,2,2,48,1536]{4,3,2,1,0:T(8,128)(2,1)S(1)} %copy-done.23, bf16[1,2,2,48,1536]{4,3,2,1,0:T(8,128)(2,1)} %bitcast.36, pred[]{:T(512)S(6)} %eq.40), kind=kLoop, calls=%fused_computation.49 | loop fusion | flops 1769472 | bytes 2359297 | tf_op jit(solution)/shard_map/jit(_where)/select_n | solution.py:311
  54.3 2.5 %maximum_select_fusion.5 = bf16[1,2,2,2,48,1536]{5,4,3,2,1,0:T(8,128)(2,1)} fusion(bf16[1,1,2,2,48,1536]{5,4,3,2,1,0:T(8,128)(2,1)S(1)} %copy-done.22, bf16[1,1,2,2,48,1536]{5,4,3,2,1,0:T(8,128)(2,1)} %bitcast.41, pred[]{:T(512)S(6)} %eq.40), kind=kLoop, calls=%fused_computation.50 | loop fusion | flops 1769472 | bytes 2359297 | tf_op jit(solution)/shard_map/jit(_where)/select_n | solution.py:311
  58.3 2.2 fusion.101.xp_ref
  60.5 2.1 copy-done.39
  64.7 12.8 %scan_forward.1 = (f32[1024,768]{1,0:T(8,128)S(1)}, f32[1024,1024]{1,0:T(8,128)S(1)}, bf16[4,128,768]{2,1,0:T(8,128)(2,1)S(1)}) custom-call(f32[1024,1152]{1,0:T(8,128)} %copy-done.39, f32[1024,128]{1,0:T(8,128)S(1)} %pad.17.clone.col_ref, f32[32,1024]{1,0:T(8,128)S(1)} %get-tuple-element.133.row_ref, f32[8,1024]{1,0:T(8,128)S(1)} %maximum_maximum_fusion.w_ref, ...), custom_call_target="tpu_custom_call" | custom-call | flops 20000000000 | bytes 13000000 | tf_op jit(solution)/shard_map/scan_forward/pallas_call | solution.py:198
  78.5 3.5 %fusion.8 = bf16[2,2,2,2,48,1536]{5,4,2,0,1,3:T(8,128)(2,1)S(1)} fusion(bf16[1,2,2,2,48,1536]{5,4,3,2,1,0:T(8,128)(2,1)S(1)} %copy-done.15, bf16[1,2,2,2,48,1536]{5,4,3,2,1,0:T(8,128)(2,1)} %bitcast.40, pred[]{:T(512)S(6)} %eq.38), kind=kLoop, calls=%fused_computation.25 | loop fusion | flops 3538944 | bytes 4718593 | tf_op jit(solution)/shard_map/transpose | solution.py:323
  85.5 4.2 %multiply_reduce_fusion.2 = (f32[1024]{0:T(1024)S(1)}, f32[1024]{0:T(1024)S(1)}, f32[1024,768]{1,0:T(8,128)}, f32[1024,768]{1,0:T(8,128)}) fusion(f32[768]{0:T(1024)S(1)} %copy-done.41, f32[1024,768]{1,0:T(8,128)S(1)} %get-tuple-element.40, f32[1024,768]{1,0:T(8,128)S(1)} %fusion.26, bf16[1024,768]{1,0:T(8,128)(2,1)S(1)} %bitcast.255, ...), kind=kOutput, calls=%fused_computation.18 | convolution fusion | flops 1215821824 | bytes 15347712 | tf_op jit(solution)/shard_map/dot_general | solution.py:23
  93.5 6.2 %multiply_convert_fusion = (bf16[1024,768]{1,0:T(8,128)(2,1)S(1)}, bf16[1024,768]{1,0:T(8,128)(2,1)S(1)}, f32[768]{0:T(1024)S(1)}, bf16[1024,768]{1,0:T(8,128)(2,1)S(1)}) fusion(f32[1024,768]{1,0:T(8,128)} %get-tuple-element.118, f32[1024]{0:T(1024)S(1)} %fusion.76, f32[1024,768]{1,0:T(8,128)} %get-tuple-element.162, f32[1024]{0:T(1024)S(1)} %bitcast.299, ...), kind=kLoop, calls=%fused_computation.13 | loop fusion | flops 18087168 | bytes 17315840 | tf_op jit(solution)/shard_map/convert_element_type | solution.py:417
  99.7 3.1 %fusion.24 = f32[1024,768]{1,0:T(8,128)} fusion(bf16[1024,768]{1,0:T(8,128)(2,1)S(1)} %get-tuple-element.122, bf16[768,1536]{1,0:T(8,128)(2,1)S(1)} %bitcast.264), kind=kOutput, calls=%fused_computation.64 | convolution fusion | flops 1207959552 | bytes 5898240 | tf_op jit(solution)/shard_map/dot_general | solution.py:23
  111.8 8.0 %scan_backward.3 = (bf16[1024,768]{1,0:T(8,128)(2,1)S(1)}, bf16[1024,256]{1,0:T(8,128)(2,1)S(1)}, f32[1024,128]{1,0:T(8,128)S(1)}, f32[16,1024]{1,0:T(8,128)S(1)...) custom-call(f32[1024,1152]{1,0:T(8,128)} %copy-done.39, ...), custom_call_target="tpu_custom_call" | custom-call | flops 8000000000 | bytes 4000000 | tf_op jit(solution)/shard_map/scan_backward/pallas_call | solution.py:245
  119.7 8.1 %collective-permute-done.11 = bf16[512,768]{1,0:T(8,128)(2,1)S(1)} collective-permute-done((bf16[512,768]{1,0:T(8,128)(2,1)}, bf16[512,768]{1,0:T(8,128)(2,1)S(1)}, u32[]{:S(2)}, u32[]{:S(2)}) %collective-permute-start.11) | collective-permute-done | bytes 786464 | tf_op jit(solution)/shard_map/ppermute | solution.py:298
  132.9 14.8 %scan_backward.4 = (bf16[1024,768]{1,0:T(8,128)(2,1)S(1)}, bf16[1024,256]{1,0:T(8,128)(2,1)S(1)}, f32[1024,128]{1,0:T(8,128)S(1)}, f32[16,1024]{1,0:T(8,128)S(1)...) custom-call(f32[1024,1152]{1,0:T(8,128)} %copy-done.39, ...), custom_call_target="tpu_custom_call", output_to_operand_aliasing={{0}: (11, {}), {1}: (12, {}), {2}: (13, {}), {3}: (14, {}),... | custom-call | flops 16000000000 | bytes 8000000 | tf_op jit(solution)/shard_map/scan_backward/pallas_call | solution.py:245
  149.5 8.6 %scan_backward.5 = (bf16[1024,768]{1,0:T(8,128)(2,1)S(1)}, bf16[1024,256]{1,0:T(8,128)(2,1)S(1)}, f32[1024,128]{1,0:T(8,128)S(1)}, f32[16,1024]{1,0:T(8,128)S(1)...) custom-call(f32[1024,1152]{1,0:T(8,128)} %copy-done.39, ...), custom_call_target="tpu_custom_call", output_to_operand_aliasing={{0}: (11, {}), {1}: (12, {}), {2}: (13, {}), {3}: (14, {}),... | custom-call | flops 8000000000 | bytes 4000000 | tf_op jit(solution)/shard_map/scan_backward/pallas_call | solution.py:245
  158.1 2.8 %fusion.14 = f32[2,2,2,2,48,768]{5,4,3,2,1,0:T(8,128)} fusion(bf16[2,2,2,2,48,1024]{5,4,3,2,1,0:T(8,128)(2,1)S(1)} %bitcast.275, bf16[1024,768]{1,0:T(8,128)(2,1)S(1)} %get-tuple-element.59), kind=kOutput, calls=%fused_computation.37 | convolution fusion | flops 1207959552 | bytes 5505024 | tf_op jit(solution)/shard_map/dot_general | solution.py:23
  160.9 3.1 %fusion.21 = f32[1024,768]{1,0:T(8,128)} fusion(bf16[1024,768]{1,0:T(8,128)(2,1)S(1)} %get-tuple-element.59, bf16[768,1152]{1,0:T(8,128)(2,1)S(1)} %bitcast.271), kind=kOutput, calls=%fused_computation.47 | convolution fusion | flops 1207959552 | bytes 5898240 | tf_op jit(solution)/shard_map/dot_general | solution.py:23
  174.9 4.5 %collective-permute-done.22 = bf16[48,1536]{1,0:T(8,128)(2,1)S(1)} collective-permute-done((bf16[48,1536]{1,0:T(8,128)(2,1)S(1)}, bf16[48,1536]{1,0:T(8,128)(2,1)S(1)}, u32[]{:S(2)}, u32[]{:S(2)}) %collective-permute-start.22) | collective-permute-done | bytes 147488 | tf_op jit(solution)/shard_map/ppermute | solution.py:298
  182.3 5.1 %fusion.6 = (f32[768]{0:T(1024)S(1)}, f32[1024,768]{1,0:T(8,128)}) fusion(f32[1024]{0:T(1024)S(1)} %bitcast.303, bf16[1,512,768]{2,1,0:T(8,128)(2,1)S(1)} %bitcast.252, bf16[1,512,768]{2,1,0:T(8,128)(2,1)S(1)} %bitcast.248, pred[]{:T(512)S(6)} %eq.37, bf16[768,1152]{1,0:T(8,128)(2,1)} %bitcast.270, bf16[1024,256]{1,0:T(8,128)(2,1)S(1)} %get-tuple-element.116, ...), kind=kOutput, calls=%fused_computation.10 | convolution fusion | flops 613416192 | bytes 12155905 | tf_op jit(solution)/shard_map/dot_general | solution.py:23
  188.2 2.0 fusion.37
  194.2 2.2 collective-permute-done.18
  196.5 2.4 %dynamic-slice_convert_fusion = bf16[512,768]{1,0:T(8,128)(2,1)} fusion(f32[1024,768]{1,0:T(8,128)} %get-tuple-element.164, s32[]{:T(128)S(6)} %select_n.356), kind=kLoop, calls=%fused_computation.44 | loop fusion | bytes 1572868 | tf_op jit(solution)/shard_map/convert_element_type | solution.py:463
  202.3 3.2 %collective-permute-done.20 = f32[56,128]{1,0:T(8,128)S(1)} collective-permute-done((f32[56,128]{1,0:T(8,128)S(1)}, f32[56,128]{1,0:T(8,128)S(1)}, u32[]{:S(2)}, u32[]{:S(2)}) %collective-permute-start.20) | collective-permute-done | bytes 28704 | tf_op jit(solution)/shard_map/ppermute | solution.py:298
  210.8 8.3 %collective-permute-done.15 = bf16[512,768]{1,0:T(8,128)(2,1)S(1)} collective-permute-done((bf16[512,768]{1,0:T(8,128)(2,1)}, bf16[512,768]{1,0:T(8,128)(2,1)S(1)}, u32[]{:S(2)}, u32[]{:S(2)}) %collective-permute-start.15) | collective-permute-done | bytes 786464 | tf_op jit(solution)/shard_map/ppermute | solution.py:298
  221.2 4.5 %collective-permute-done.25 = bf16[2,48,1152]{2,1,0:T(8,128)(2,1)S(1)} collective-permute-done((bf16[2,48,1152]{2,1,0:T(8,128)(2,1)S(1)}, bf16[2,48,1152]{2,1,0:T(8,128)(2,1)S(1)}, u32[]{:S(2)}, u32[]{:S(2)}) %collective-permute-start.25) | collective-permute-done | bytes 221216 | tf_op jit(solution)/shard_map/ppermute | solution.py:298
  225.8 3.4 %collective-permute-start.26 = (bf16[48,1152]{1,0:T(8,128)(2,1)S(1)}, bf16[48,1152]{1,0:T(8,128)(2,1)S(1)}, u32[]{:S(2)}, u32[]{:S(2)}) collective-permute-start(bf16[48,1152]{1,0:T(8,128)(2,1)S(1)} %fusion.67), channel_id=1, source_target_pairs={{0,16},{2,18},{4,20},{6,22},{8,24},{10,26},{12,28},{14,30},{16,0},... | collective-permute-start | bytes 331784 | tf_op jit(solution)/shard_map/ppermute | solution.py:298
  230.7 2.4 %collective-permute-done.26 = bf16[48,1152]{1,0:T(8,128)(2,1)S(1)} collective-permute-done((bf16[48,1152]{1,0:T(8,128)(2,1)S(1)}, bf16[48,1152]{1,0:T(8,128)(2,1)S(1)}, u32[]{:S(2)}, u32[]{:S(2)}) %collective-permute-start.26) | collective-permute-done | bytes 110624 | tf_op jit(solution)/shard_map/ppermute | solution.py:298
  (284 shorter events, 80.6 us)
Async XLA Ops:
  3.2 9.5 %collective-permute-start.1 = (bf16[48,1152]{1,0:T(8,128)(2,1)S(1)}, bf16[48,1152]{1,0:T(8,128)(2,1)S(1)}, u32[]{:S(2)}, u32[]{:S(2)}) collective-permute-start(bf16[48,1152]{1,0:T(8,128)(2,1)S(1)} %fusion.66), channel_id=1, source_target_pairs={{0,16},{2,18},{4,20},{6,22},{8,24},{10,26},{12,28},{14,30},{16,0},... | collective-permute-start | bytes 331784 | tf_op jit(solution)/shard_map/ppermute | solution.py:298
  7.3 28.0 %collective-permute-start = (bf16[512,768]{1,0:T(8,128)(2,1)}, bf16[512,768]{1,0:T(8,128)(2,1)S(1)}, u32[]{:S(2)}, u32[]{:S(2)}) collective-permute-start(bf16[512,768]{1,0:T(8,128)(2,1)} %param.15), channel_id=1, source_target_pairs={{0,1},{1,0},{2,3},{3,2},{4,5},{5,4},{6,7},{7,6},{8,9},{9,8},{10,11... | collective-permute-start | bytes 2359304 | tf_op jit(solution)/shard_map/ppermute | solution.py:298
  9.7 5.2 %collective-permute-start.5 = (bf16[48,1536]{1,0:T(8,128)(2,1)S(1)}, bf16[48,1536]{1,0:T(8,128)(2,1)S(1)}, u32[]{:S(2)}, u32[]{:S(2)}) collective-permute-start(bf16[48,1536]{1,0:T(8,128)(2,1)S(1)} %get-tuple-element.139), channel_id=1, source_target_pairs={{0,4},{2,6},{4,0},{6,2},{8,12},{10,14},{12,8},{14,10},{16,20},{18,... | collective-permute-start | bytes 442376 | tf_op jit(solution)/shard_map/ppermute | solution.py:298
  11.3 32.2 %collective-permute-start.9 = (bf16[512,768]{1,0:T(8,128)(2,1)}, bf16[512,768]{1,0:T(8,128)(2,1)}, u32[]{:S(2)}, u32[]{:S(2)}) collective-permute-start(bf16[512,768]{1,0:T(8,128)(2,1)} %param.16), channel_id=1, source_target_pairs={{0,1},{1,0},{2,3},{3,2},{4,5},{5,4},{6,7},{7,6},{8,9},{9,8},{10,11... | collective-permute-start | bytes 2359304 | tf_op jit(solution)/shard_map/ppermute | solution.py:298
  12.1 50.8 %copy-start.46 = (f32[12]{0:T(128)}, f32[12]{0:T(128)S(1)}, u32[]{:S(2)}) copy-start(f32[12]{0:T(128)S(1)} %exponential_negate_fusion) | copy-start | bytes 148
  12.8 11.0 %collective-permute-start.2 = (bf16[2,48,1152]{2,1,0:T(8,128)(2,1)S(1)}, bf16[2,48,1152]{2,1,0:T(8,128)(2,1)S(1)}, u32[]{:S(2)}, u32[]{:S(2)}) collective-permute-start(bf16[2,48,1152]{2,1,0:T(8,128)(2,1)S(1)} %maximum_select_fusion.13), channel_id=1, source_target_pairs={{0,8},{2,10},{4,12},{6,14},{8,0},{10,2},{12,4},{14,6},{16,24},{18,... | collective-permute-start | bytes 663560 | tf_op jit(solution)/shard_map/ppermute | solution.py:298
  15.0 15.4 %collective-permute-start.6 = (bf16[2,48,1536]{2,1,0:T(8,128)(2,1)S(1)}, bf16[2,48,1536]{2,1,0:T(8,128)(2,1)S(1)}, u32[]{:S(2)}, u32[]{:S(2)}) collective-permute-start(bf16[2,48,1536]{2,1,0:T(8,128)(2,1)S(1)} %maximum_select_fusion.11), channel_id=1, source_target_pairs={{0,16},{2,18},{4,20},{6,22},{8,24},{10,26},{12,28},{14,30},{16,0},... | collective-permute-start | bytes 884744 | tf_op jit(solution)/shard_map/ppermute | solution.py:298
  23.8 9.3 %collective-permute-start.3 = (bf16[2,2,48,1152]{3,2,0,1:T(8,128)(2,1)S(1)}, bf16[2,2,48,1152]{3,2,0,1:T(8,128)(2,1)S(1)}, u32[]{:S(2)}, u32[]{:S(2)}) collective-permute-start(bf16[2,2,48,1152]{3,2,0,1:T(8,128)(2,1)S(1)} %maximum_select_fusion.10), channel_id=1, source_target_pairs={{0,4},{2,6},{4,0},{6,2},{8,12},{10,14},{12,8},{14,10},{16,20},{18,... | collective-permute-start | bytes 1327112 | tf_op jit(solution)/shard_map/ppermute | solution.py:298
  31.3 19.9 %collective-permute-start.7 = (bf16[2,2,48,1536]{3,2,1,0:T(8,128)(2,1)}, bf16[2,2,48,1536]{3,2,1,0:T(8,128)(2,1)}, u32[]{:S(2)}, u32[]{:S(2)}) collective-permute-start(bf16[2,2,48,1536]{3,2,1,0:T(8,128)(2,1)} %maximum_select_fusion.8), channel_id=1, source_target_pairs={{0,8},{2,10},{4,12},{6,14},{8,0},{10,2},{12,4},{14,6},{16,24},{18,... | collective-permute-start | bytes 1769480 | tf_op jit(solution)/shard_map/ppermute | solution.py:298
  34.3 22.5 %collective-permute-start.4 = (bf16[2,2,2,48,1152]{4,3,1,2,0:T(8,128)(2,1)}, bf16[2,2,2,48,1152]{4,3,1,2,0:T(8,128)(2,1)}, u32[]{:S(2)}, u32[]{:S(2)}) collective-permute-start(bf16[2,2,2,48,1152]{4,3,1,2,0:T(8,128)(2,1)} %maximum_select_fusion.6), channel_id=1, source_target_pairs={{0,2},{2,0},{4,6},{6,4},{8,10},{10,8},{12,14},{14,12},{16,18},{18,... | collective-permute-start | bytes 2654216 | tf_op jit(solution)/shard_map/ppermute | solution.py:298
  35.3 15.4 %copy-start.9 = (bf16[512,768]{1,0:T(8,128)(2,1)}, bf16[512,768]{1,0:T(8,128)(2,1)S(1)}, u32[]{:S(2)}) copy-start(bf16[512,768]{1,0:T(8,128)(2,1)S(1)} %collective-permute-done) | copy-start | bytes 2359300
  54.2 24.2 %collective-permute-start.8 = (bf16[2,2,2,48,1536]{4,3,2,1,0:T(8,128)(2,1)}, bf16[2,2,2,48,1536]{4,3,2,1,0:T(8,128)(2,1)}, u32[]{:S(2)}, u32[]{:S(2)}) collective-permute-start(bf16[2,2,2,48,1536]{4,3,2,1,0:T(8,128)(2,1)} %maximum_select_fusion.4._), channel_id=1, source_target_pairs={{0,2},{2,0},{4,6},{6,4},{8,10},{10,8},{12,14},{14,12},{16,18},{18,... | collective-permute-start | bytes 3538952 | tf_op jit(solution)/shard_map/ppermute | solution.py:298
  64.7 12.8 %copy-start = (f32[1024,128]{1,0:T(8,128)}, f32[1024,128]{1,0:T(8,128)S(1)}, u32[]{:S(2)}) copy-start(f32[1024,128]{1,0:T(8,128)S(1)} %pad.17.clone.col_ref) | copy-start | bytes 1572868
  64.7 13.7 %copy-start.15 = (bf16[1,2,2,2,48,1536]{5,4,3,2,1,0:T(8,128)(2,1)S(1)}, bf16[1,2,2,2,48,1536]{5,4,3,2,1,0:T(8,128)(2,1)}, u32[]{:S(2)}) copy-start(bf16[1,2,2,2,48,1536]{5,4,3,2,1,0:T(8,128)(2,1)} %maximum_select_fusion.5) | copy-start | bytes 3538948
  89.7 3.7 %collective-permute-start.10 = (f32[2,1024]{1,0:T(2,128)S(1)}, f32[2,1024]{1,0:T(2,128)S(1)}, u32[]{:S(2)}, u32[]{:S(2)}) collective-permute-start(f32[2,1024]{1,0:T(2,128)S(1)} %pad_maximum_fusion.8), channel_id=1, source_target_pairs={{0,1},{1,0},{2,3},{3,2},{4,5},{5,4},{6,7},{7,6},{8,9},{9,8},{10,11... | collective-permute-start | bytes 24584 | tf_op jit(solution)/shard_map/ppermute | solution.py:298
  105.9 23.7 %collective-permute-start.12 = (bf16[2,2,2,48,1536]{4,3,0,1,2:T(8,128)(2,1)S(1)}, bf16[2,2,2,48,1536]{4,3,0,1,2:T(8,128)(2,1)}, u32[]{:S(2)}, u32[]{:S(2)}) collective-permute-start(bf16[2,2,2,48,1536]{4,3,0,1,2:T(8,128)(2,1)S(1)} %pad_maximum_fusion), channel_id=1, source_target_pairs={{0,2},{2,0},{4,6},{6,4},{8,10},{10,8},{12,14},{14,12},{16,18},{18,... | collective-permute-start | bytes 3538952 | tf_op jit(solution)/shard_map/ppermute | solution.py:298
  107.7 20.1 %collective-permute-start.11 = (bf16[512,768]{1,0:T(8,128)(2,1)}, bf16[512,768]{1,0:T(8,128)(2,1)S(1)}, u32[]{:S(2)}, u32[]{:S(2)}) collective-permute-start(bf16[512,768]{1,0:T(8,128)(2,1)} %convolution_convert_fusion), channel_id=1, source_target_pairs={{0,1},{1,0},{2,3},{3,2},{4,5},{5,4},{6,7},{7,6},{8,9},{9,8},{10,11... | collective-permute-start | bytes 2359304 | tf_op jit(solution)/shard_map/ppermute | solution.py:298
  111.8 16.0 %copy-start.7 = (bf16[512,768]{1,0:T(8,128)(2,1)S(1)}, bf16[512,768]{1,0:T(8,128)(2,1)}, u32[]{:S(2)}) copy-start(bf16[512,768]{1,0:T(8,128)(2,1)} %param.15) | copy-start | bytes 2359300
  131.3 16.4 %collective-permute-start.13 = (bf16[2,2,48,1536]{3,2,0,1:T(8,128)(2,1)S(1)}, bf16[2,2,48,1536]{3,2,0,1:T(8,128)(2,1)S(1)}, u32[]{:S(2)}, u32[]{:S(2)}) collective-permute-start(bf16[2,2,48,1536]{3,2,0,1:T(8,128)(2,1)S(1)} %fusion.43), channel_id=1, source_target_pairs={{0,4},{2,6},{4,0},{6,2},{8,12},{10,14},{12,8},{14,10},{16,20},{18,... | collective-permute-start | bytes 1769480 | tf_op jit(solution)/shard_map/ppermute | solution.py:298
  147.9 21.0 %collective-permute-start.21 = (bf16[2,48,1536]{2,1,0:T(8,128)(2,1)S(1)}, bf16[2,48,1536]{2,1,0:T(8,128)(2,1)}, u32[]{:S(2)}, u32[]{:S(2)}) collective-permute-start(bf16[2,48,1536]{2,1,0:T(8,128)(2,1)S(1)} %fusion.52.refs_5_), channel_id=1, source_target_pairs={{0,8},{2,10},{4,12},{6,14},{8,0},{10,2},{12,4},{14,6},{16,24},{18,... | collective-permute-start | bytes 884744 | tf_op jit(solution)/shard_map/ppermute | solution.py:298
  167.1 13.9 %collective-permute-start.14 = (bf16[1024,256]{1,0:T(8,128)(2,1)S(1)}, bf16[1024,256]{1,0:T(8,128)(2,1)}, u32[]{:S(2)}, u32[]{:S(2)}) collective-permute-start(bf16[1024,256]{1,0:T(8,128)(2,1)S(1)} %get-tuple-element.60), channel_id=1, source_target_pairs={{0,1},{1,0},{2,3},{3,2},{4,5},{5,4},{6,7},{7,6},{8,9},{9,8},{10,11... | collective-permute-start | bytes 1572872 | tf_op jit(solution)/shard_map/ppermute | solution.py:298
  170.7 8.6 %collective-permute-start.22 = (bf16[48,1536]{1,0:T(8,128)(2,1)S(1)}, bf16[48,1536]{1,0:T(8,128)(2,1)S(1)}, u32[]{:S(2)}, u32[]{:S(2)}) collective-permute-start(bf16[48,1536]{1,0:T(8,128)(2,1)S(1)} %fusion.61), channel_id=1, source_target_pairs={{0,16},{2,18},{4,20},{6,22},{8,24},{10,26},{12,28},{14,30},{16,0},... | collective-permute-start | bytes 442376 | tf_op jit(solution)/shard_map/ppermute | solution.py:298
  187.4 3.7 %collective-permute-start.16 = (f32[2048]{0:T(1024)S(1)}, f32[2048]{0:T(1024)S(1)}, u32[]{:S(2)}, u32[]{:S(2)}) collective-permute-start(f32[2048]{0:T(1024)S(1)} %pad_maximum_fusion.9), channel_id=1, source_target_pairs={{0,1},{1,0},{2,3},{3,2},{4,5},{5,4},{6,7},{7,6},{8,9},{9,8},{10,11... | collective-permute-start | bytes 24584 | tf_op jit(solution)/shard_map/ppermute | solution.py:298
  191.3 1.2 collective-permute-start.17
  192.5 3.9 %collective-permute-start.18 = (f32[56,128]{1,0:T(8,128)S(1)}, f32[56,128]{1,0:T(8,128)S(1)}, u32[]{:S(2)}, u32[]{:S(2)}) collective-permute-start(f32[56,128]{1,0:T(8,128)S(1)} %fusion.89), channel_id=1, source_target_pairs={{0,4},{2,6},{4,0},{6,2},{8,12},{10,14},{12,8},{14,10},{16,20},{18,... | collective-permute-start | bytes 86024 | tf_op jit(solution)/shard_map/ppermute | solution.py:298
  194.1 13.2 %collective-permute-start.23 = (bf16[2,2,2,48,1152]{4,3,0,1,2:T(8,128)(2,1)}, bf16[2,2,2,48,1152]{4,3,0,1,2:T(8,128)(2,1)}, u32[]{:S(2)}, u32[]{:S(2)}) collective-permute-start(bf16[2,2,2,48,1152]{4,3,0,1,2:T(8,128)(2,1)} %pad_maximum_fusion.1), channel_id=1, source_target_pairs={{0,2},{2,0},{4,6},{6,4},{8,10},{10,8},{12,14},{14,12},{16,18},{18,... | collective-permute-start | bytes 2654216 | tf_op jit(solution)/shard_map/ppermute | solution.py:298
  196.4 3.9 %collective-permute-start.19 = (f32[56,128]{1,0:T(8,128)S(1)}, f32[56,128]{1,0:T(8,128)S(1)}, u32[]{:S(2)}, u32[]{:S(2)}) collective-permute-start(f32[56,128]{1,0:T(8,128)S(1)} %fusion.112), channel_id=1, source_target_pairs={{0,8},{2,10},{4,12},{6,14},{8,0},{10,2},{12,4},{14,6},{16,24},{18,... | collective-permute-start | bytes 86024 | tf_op jit(solution)/shard_map/ppermute | solution.py:298
  200.4 5.1 %collective-permute-start.20 = (f32[56,128]{1,0:T(8,128)S(1)}, f32[56,128]{1,0:T(8,128)S(1)}, u32[]{:S(2)}, u32[]{:S(2)}) collective-permute-start(f32[56,128]{1,0:T(8,128)S(1)} %add.274), channel_id=1, source_target_pairs={{0,16},{2,18},{4,20},{6,22},{8,24},{10,26},{12,28},{14,30},{16,0},... | collective-permute-start | bytes 86024 | tf_op jit(solution)/shard_map/ppermute | solution.py:298
  201.3 17.8 %collective-permute-start.15 = (bf16[512,768]{1,0:T(8,128)(2,1)}, bf16[512,768]{1,0:T(8,128)(2,1)S(1)}, u32[]{:S(2)}, u32[]{:S(2)}) collective-permute-start(bf16[512,768]{1,0:T(8,128)(2,1)} %dynamic-slice_convert_fusion), channel_id=1, source_target_pairs={{0,1},{1,0},{2,3},{3,2},{4,5},{5,4},{6,7},{7,6},{8,9},{9,8},{10,11... | collective-permute-start | bytes 2359304 | tf_op jit(solution)/shard_map/ppermute | solution.py:298
  209.0 10.5 %collective-permute-start.24 = (bf16[2,2,48,1152]{3,2,0,1:T(8,128)(2,1)S(1)}, bf16[2,2,48,1152]{3,2,0,1:T(8,128)(2,1)S(1)}, u32[]{:S(2)}, u32[]{:S(2)}) collective-permute-start(bf16[2,2,48,1152]{3,2,0,1:T(8,128)(2,1)S(1)} %fusion.49), channel_id=1, source_target_pairs={{0,4},{2,6},{4,0},{6,2},{8,12},{10,14},{12,8},{14,10},{16,20},{18,... | collective-permute-start | bytes 1327112 | tf_op jit(solution)/shard_map/ppermute | solution.py:298
  219.7 6.0 %collective-permute-start.25 = (bf16[2,48,1152]{2,1,0:T(8,128)(2,1)S(1)}, bf16[2,48,1152]{2,1,0:T(8,128)(2,1)S(1)}, u32[]{:S(2)}, u32[]{:S(2)}) collective-permute-start(bf16[2,48,1152]{2,1,0:T(8,128)(2,1)S(1)} %fusion.58), channel_id=1, source_target_pairs={{0,8},{2,10},{4,12},{6,14},{8,0},{10,2},{12,4},{14,6},{16,24},{18,... | collective-permute-start | bytes 663560 | tf_op jit(solution)/shard_map/ppermute | solution.py:298
  225.8 7.4 %collective-permute-start.26 = (bf16[48,1152]{1,0:T(8,128)(2,1)S(1)}, bf16[48,1152]{1,0:T(8,128)(2,1)S(1)}, u32[]{:S(2)}, u32[]{:S(2)}) collective-permute-start(bf16[48,1152]{1,0:T(8,128)(2,1)S(1)} %fusion.67), channel_id=1, source_target_pairs={{0,16},{2,18},{4,20},{6,22},{8,24},{10,26},{12,28},{14,30},{16,0},... | collective-permute-start | bytes 331784 | tf_op jit(solution)/shard_map/ppermute | solution.py:298
  (47 other events, 246.3 us)
